TPU v7x, 32 devices: a whole 2x2x4 slice. The times are simulated.
32 devices in a mesh: leaf: 4 (over y, x), row: 4 (over z), col: 2 (over core).
Axes of the slice: x: 2, y: 2, z: 4, core: 2. Of those that a mesh axis runs over, the one named last changes fastest.
Arguments:
- rhs_leaf: bfloat16 [4, 12288, 256], P('leaf', 'col'), may hold values from -6 to 6
- rhs_parent: bfloat16 [16384, 256], P(('leaf', 'row', 'col')), may hold values from -6 to 6
- inv_leaf: bfloat16 [4, 12288, 12288], P('leaf', 'row', 'col'), as said below
- panel: bfloat16 [4, 6144, 12288], P('leaf', 'col', 'row'), may hold values from -0.0546875 to 0.0546875
- row_map: int32 [4, 6144], P('leaf', 'col'), may hold values from 0 to 16383, as said below
- inv_parent: bfloat16 [16384, 16384], P(('row', 'col'), 'leaf'), as said below
Outputs:
- sol_leaf: bfloat16 [4, 12288, 256], P('leaf', 'col')
- sol_parent: bfloat16 [16384, 256], P(('leaf', 'row', 'col'))
Inputs may be any that keep to these rules, and one draw needn't show every extreme that they name: Within one leaf the 6144 entries of row_map are distinct parent rows. Split the parent rows into 32 owner blocks of 16384 // 32 consecutive rows: in each aligned block of 768 consecutive entries of a leaf, at most 24 entries fall in one owner block, and exactly 24 in some. `inv_leaf`: lower triangular: zeros above the diagonal, diagonal entries between 0.5 and 2. `inv_parent`: lower triangular: zeros above the diagonal, diagonal entries between 0.5 and 2.
All inputs are finite; a program needn't handle non-finite values.
Results may differ from a plain program's by a relative error of at most 0.01.
Values may be sent and summed in bfloat16 or wider, within the bound.
No kernel may reach another device: no remote copies, remote signals or barrier semaphores. Data moves between devices by JAX's collectives and lax.ppermute only.
A program may use at most 192 MiB of HBM per device.

v0:
```python
import jax
import jax.experimental.pallas as pl
import jax.experimental.pallas.tpu as pltpu
import jax.numpy as jnp
from jax import lax
from jax.sharding import PartitionSpec as P

ALL = ("leaf", "row", "col")
F32 = jnp.float32
BF16 = jnp.bfloat16
CHUNKS = 12
GROUP = 2
VMEM = 40 * 2**20


def matmul(a, x):
    return jnp.dot(a, x, preferred_element_type=F32)


def matmul_t(a, x):
    return lax.dot_general(a, x, (((0,), (0,)), ((), ())), preferred_element_type=F32)


def sum_cores(part):
    if lax.axis_size("col") == 2:
        other = lax.ppermute(part.astype(BF16), "col", [(0, 1), (1, 0)])
        return part + other.astype(F32)
    return lax.psum(part, "col")


def swap_leaves(halves, steps):
    size = lax.axis_size("leaf")
    bits = [1 << b for b in range(size.bit_length() - 1)]
    orders = (bits, bits[::-1])
    for step in range(len(bits))[steps]:
        moved = [
            lax.ppermute(h.astype(BF16), "leaf", [(i, i ^ order[step]) for i in range(size)])
            for h, order in zip(halves, orders)
        ]
        halves = [h + m.astype(F32) for h, m in zip(halves, moved)]
    return halves


def gather_lists(local):
    size = lax.axis_size("leaf")
    parts = [local] + [
        lax.ppermute(local, "leaf", [(i, i ^ d) for i in range(size)]) for d in range(1, size)
    ]
    order = lax.axis_index("leaf") ^ jnp.arange(size)
    lists = jnp.take(jnp.stack(parts), order, axis=0, mode="clip")
    if lax.axis_size("col") == 2:
        c = lax.axis_index("col")
        other = lax.ppermute(lists, "col", [(0, 1), (1, 0)])
        return jnp.stack([jnp.where(c == 0, lists, other), jnp.where(c == 0, other, lists)], axis=1)
    return lax.all_gather(lists, "col", axis=1)


def gather_block(own):
    depth = lax.axis_size("row")
    z = lax.axis_index("row")
    parts = [own] + [
        lax.ppermute(own, "row", [(i, (i + d) % depth) for i in range(depth)])
        for d in range(1, depth)
    ]
    cores = lax.axis_size("col")
    if cores == 2:
        c = lax.axis_index("col")
        parts += [lax.ppermute(part, "col", [(0, 1), (1, 0)]) for part in parts]
        place = jnp.arange(depth * cores)
        source = (z - place // cores) % depth + depth * ((place % cores) ^ c)
    else:
        parts = [lax.all_gather(jnp.stack(parts), "col", axis=1)]
        place = jnp.arange(depth * cores)
        source = (z - place // cores) % depth * cores + place % cores
    parts = jnp.stack(parts).reshape(depth * cores, *own.shape)
    return jnp.take(parts, source, axis=0, mode="clip").reshape(-1, own.shape[1])


def columns_t(a, x, depth, cores):
    k, m = a.shape
    rows = m // (depth * cores)
    width = x.shape[1]
    which = jnp.stack([lax.axis_index("col"), lax.axis_index("row")]).astype(jnp.int32)

    def kernel(which_ref, a_ref, x_ref, out_ref):
        for e in range(cores):
            core = lax.rem(which_ref[0] + 1 + e, cores)
            cols = pl.ds(pl.multiple_of(core * rows, rows), rows)
            out_ref[e, 0] = matmul_t(a_ref[:, cols], x_ref[...]).astype(BF16)

    return pl.pallas_call(
        kernel,
        grid_spec=pltpu.PrefetchScalarGridSpec(
            num_scalar_prefetch=1,
            grid=(depth,),
            in_specs=[
                pl.BlockSpec(
                    (k, cores * rows),
                    lambda d, which_ref: (0, lax.rem(which_ref[1] + d, depth)),
                ),
                pl.BlockSpec((k, width), lambda d, which_ref: (0, 0)),
            ],
            out_specs=pl.BlockSpec((cores, 1, rows, width), lambda d, which_ref: (0, d, 0, 0)),
        ),
        out_shape=jax.ShapeDtypeStruct((cores, depth, rows, width), BF16),
        compiler_params=pltpu.CompilerParams(vmem_limit_bytes=VMEM),
        cost_estimate=pl.CostEstimate(
            flops=2 * k * m * width, bytes_accessed=2 * k * m, transcendentals=0
        ),
    )(which, a, x)


def dot_t(a, x, first, count, tile, dtype):
    k = a.shape[0]
    width = x.shape[1]

    def kernel(a_ref, x_ref, *out_refs):
        part = matmul_t(a_ref[...], x_ref[...]).astype(dtype)
        for j, out_ref in enumerate(out_refs):

            @pl.when(pl.program_id(0) == j)
            def _():
                out_ref[...] = part

    return pl.pallas_call(
        kernel,
        grid=(count,),
        in_specs=[
            pl.BlockSpec((k, tile), lambda i: (0, first + i)),
            pl.BlockSpec((k, width), lambda i: (0, 0)),
        ],
        out_specs=[pl.BlockSpec((tile, width), lambda i: (0, 0))] * count,
        out_shape=[jax.ShapeDtypeStruct((tile, width), dtype)] * count,
        compiler_params=pltpu.CompilerParams(vmem_limit_bytes=VMEM),
        cost_estimate=pl.CostEstimate(
            flops=2 * k * count * tile * width,
            bytes_accessed=2 * k * count * tile,
            transcendentals=0,
        ),
    )(a, x)


def matmul_t_tiled(a, x):
    k, m = a.shape
    width = x.shape[1]
    tile = min(m, 1024)

    def kernel(a_ref, x_ref, out_ref):
        out_ref[...] = matmul_t(a_ref[...], x_ref[...])

    return pl.pallas_call(
        kernel,
        grid=(m // tile,),
        in_specs=[
            pl.BlockSpec((k, tile), lambda i: (0, i)),
            pl.BlockSpec((k, width), lambda i: (0, 0)),
        ],
        out_specs=pl.BlockSpec((tile, width), lambda i: (i, 0)),
        out_shape=jax.ShapeDtypeStruct((m, width), F32),
        compiler_params=pltpu.CompilerParams(vmem_limit_bytes=VMEM),
        cost_estimate=pl.CostEstimate(
            flops=2 * k * m * width, bytes_accessed=2 * k * m, transcendentals=0
        ),
    )(a, x)


def solve_and_swap(a, x):
    cores = lax.axis_size("col")
    parts = columns_t(a, x, lax.axis_size("row"), cores)
    total = parts[-1]
    for e in range(cores - 1):
        total = total + lax.ppermute(
            parts[e], "col", [(i, (i + 1 + e) % cores) for i in range(cores)]
        )
    return total


def scatter_rows(summed):
    depth = lax.axis_size("row")
    total = summed[0].astype(F32)
    for d in range(1, depth):
        moved = lax.ppermute(summed[d], "row", [(i, (i + d) % depth) for i in range(depth)])
        total = total + moved.astype(F32)
    return total.astype(BF16)


def solve_and_sum_rows(inverse, x):
    depth = lax.axis_size("row")
    if depth != 4:
        return lax.psum(matmul_t(inverse, x), "row").astype(BF16)
    width = inverse.shape[1]
    size = width // CHUNKS
    z = lax.axis_index("row")
    inner = (z == 1) | (z == 2)
    ends = [(0, 1), (1, 0), (2, 3), (3, 2)]
    middle = [(1, 2), (2, 1)]

    def group(first, x):
        return dot_t(inverse, x, first, GROUP, size, BF16)

    total = jnp.zeros((width, x.shape[1]), BF16)
    own, outer_got, middle_got = list(group(0, x)), [], []
    for step in range(CHUNKS + 4):
        late = step - 4
        if late >= 0 and step < CHUNKS:
            send = jnp.where(inner, own[late] + middle_got[late], own[step])
        elif late >= 0:
            send = own[late] + middle_got[late]
        else:
            send = own[step]
        mid = step - 2
        if 0 <= mid < CHUNKS:
            both = own[mid] + outer_got[mid]
            send, both, outer_got[mid] = lax.optimization_barrier((send, both, outer_got[mid]))
            middle_got.append(lax.ppermute(both, "row", middle))
        if len(own) < CHUNKS and step >= len(own) - 1:
            x, send = lax.optimization_barrier((x, send))
            own.extend(group(len(own), x))
        outer_got.append(lax.ppermute(send, "row", ends))
        if late >= 0:
            others = jnp.where(
                inner,
                outer_got[late].astype(F32) + middle_got[late].astype(F32),
                outer_got[step].astype(F32),
            )
            done = (own[late].astype(F32) + others).astype(BF16)
            total = lax.dynamic_update_slice_in_dim(total, done, late * size, 0)
    return total


def slots_of(row_map, own, devices, depth):
    blocks = row_map.reshape(depth, -1)
    size = blocks.shape[1]
    cap = -(-size // devices)
    owner = blocks // own
    earlier = jnp.arange(size)[None, :] < jnp.arange(size)[:, None]
    rank = jnp.sum((owner[:, :, None] == owner[:, None, :]) & earlier[None], axis=2, dtype=jnp.int32)
    slot = owner * cap + rank
    hit = slot[:, None, :] == jnp.arange(devices * cap, dtype=jnp.int32)[None, :, None]
    local = jnp.max(jnp.where(hit, (blocks % own)[:, None, :], -1), axis=2)
    local = local.reshape(depth, devices, cap).transpose(1, 0, 2).reshape(devices, depth * cap)
    return hit.astype(BF16), local


def per_device(rhs_leaf, rhs_parent, inv_leaf, panel, row_map, inv_parent):
    leaves, depth, cores = (lax.axis_size(a) for a in ALL)
    devices = leaves * depth * cores
    me = lax.axis_index(ALL)
    own, width = rhs_parent.shape

    pick, local = slots_of(row_map[0], own, devices, depth)
    per_owner = local.shape[1]
    cap = per_owner // depth
    lists = gather_lists(local)
    mine = lax.dynamic_index_in_dim(lists, me, 2, keepdims=False).reshape(-1)
    place = (mine[None, :] == jnp.arange(own, dtype=jnp.int32)[:, None]).astype(BF16)

    forward = sum_cores(matmul(inv_leaf[0], rhs_leaf[0])).astype(BF16)
    update = matmul(panel[0], forward).astype(BF16).reshape(depth, -1, width)
    packed = jnp.einsum("bsi,bir->bsr", pick, update, preferred_element_type=F32).astype(BF16)
    packed = packed.reshape(depth, devices, cap, width).transpose(1, 0, 2, 3)
    packed = packed.reshape(devices * per_owner, width)

    arrived = lax.all_to_all(packed, ALL, 0, 0, tiled=True)
    arrived = arrived.reshape(leaves, depth, cores * per_owner, width).astype(F32).sum(1)
    arrived = arrived.reshape(leaves * cores * per_owner, width).astype(BF16)
    reduced = (rhs_parent.astype(F32) - matmul(place, arrived)).astype(BF16)

    whole = gather_block(reduced)
    halves = swap_leaves(jnp.split(matmul(inv_parent, whole), 2, axis=0), slice(0, None))
    fwd_parent = jnp.concatenate(halves, axis=0).astype(BF16)
    sol_parent = scatter_rows(solve_and_swap(inv_parent, fwd_parent))

    wanted = matmul_t(place, sol_parent).astype(BF16)
    wanted = wanted.reshape(leaves, 1, cores * per_owner, width)
    wanted = jnp.broadcast_to(wanted, (leaves, depth, cores * per_owner, width))
    got = lax.all_to_all(wanted.reshape(devices * per_owner, width), ALL, 0, 0, tiled=True)
    got = got.reshape(devices, depth, cap, width).transpose(1, 0, 2, 3)
    got = got.reshape(depth, devices * cap, width)
    picked = jnp.einsum("bsi,bsr->bir", pick, got, preferred_element_type=F32).astype(BF16)
    picked = picked.reshape(panel.shape[1], width)

    coupling = sum_cores(matmul_t_tiled(panel[0], picked))
    corrected = (forward.astype(F32) - coupling).astype(BF16)
    sol_leaf = solve_and_sum_rows(inv_leaf[0], corrected)
    return (sol_leaf[None], sol_parent)


def solution(mesh):
    in_specs = (
        P("leaf", "col", None),
        P(("leaf", "row", "col"), None),
        P("leaf", "row", "col"),
        P("leaf", "col", "row"),
        P("leaf", "col"),
        P(("row", "col"), "leaf"),
    )
    out_specs = (P("leaf", "col", None), P(("leaf", "row", "col"), None))
    return jax.shard_map(
        per_device, mesh=mesh, in_specs=in_specs, out_specs=out_specs, check_vma=False
    )
```

profile of v0, /device:TPU:0, one launch (start us, length us, event | category | flops | bytes accessed | tf_op | source)
XLA Modules:
  0.0 358.1 jit_solution(9954661049445917306)
XLA Ops:
  0.7 1.9 copy-done
  2.5 18.4 %fusion.55 = (bf16[3072,256]{1,0:T(8,128)(2,1)}, f32[3072,256]{1,0:T(8,128)}) fusion(bf16[1,6144,256]{2,1,0:T(8,128)(2,1)S(1)} %copy-done, bf16[1,3072,6144]{2,1,0:T(8,128)(2,1)} %param.8), kind=kOutput, calls=%fused_computation.134 | convolution fusion | flops 9664462848 | bytes 45613056 | tf_op jit(solution)/shard_map/dot_general | solution.py:17
  22.9 2.2 convert_reduce_fusion
  26.3 9.9 %fusion.4 = bf16[3072,256]{0,1:T(8,128)(2,1)S(1)} fusion(bf16[1,3072,3072]{2,1,0:T(8,128)(2,1)} %param.9, f32[3072,256]{1,0:T(8,128)} %get-tuple-element.132, bf16[3072,256]{1,0:T(8,128)(2,1)S(1)} %collective-permute-done), kind=kOutput, calls=%fused_computation.10 | convolution fusion | flops 4834983936 | bytes 25165824 | tf_op jit(solution)/shard_map/dot_general | solution.py:17
  36.9 3.4 fusion.7
  41.7 7.0 %all-to-all-start = ((bf16[32,96,256]{2,1,0:T(8,128)(2,1)}), bf16[32,96,256]{2,1,0:T(8,128)(2,1)S(1)}, u32[]{:S(2)}, u32[]{:S(2)}) async-start(bf16[32,96,256]{2,1,0:T(8,128)(2,1)} %bitcast.16), calls=%async_computation | async-start | bytes 3145728 | tf_op jit(solution)/shard_map/all_to_all | solution.py:264
  50.6 2.7 collective-permute-start.3
  54.2 6.6 %collective-permute-done.3 = s32[32,96]{1,0:T(8,128)S(1)} collective-permute-done((s32[32,96]{1,0:T(8,128)S(1)}, s32[32,96]{1,0:T(8,128)S(1)}, u32[]{:S(2)}, u32[]{:S(2)}) %collective-permute-start.3) | collective-permute-done | bytes 12320 | tf_op jit(solution)/shard_map/ppermute | solution.py:47
  62.9 24.6 %all-to-all-done = bf16[32,96,256]{2,1,0:T(8,128)(2,1)S(1)} async-done(((bf16[32,96,256]{2,1,0:T(8,128)(2,1)}), bf16[32,96,256]{2,1,0:T(8,128)(2,1)S(1)}, u32[]{:S(2)}, u32[]{:S(2)}) %all-to-all-start) | async-done | bytes 1572896 | tf_op jit(solution)/shard_map/all_to_all | solution.py:264
  89.0 3.5 collective-permute-start.7
  92.5 7.1 %collective-permute-done.5 = bf16[512,256]{1,0:T(8,128)(2,1)S(1)} collective-permute-done((bf16[512,256]{1,0:T(8,128)(2,1)S(1)}, bf16[512,256]{1,0:T(8,128)(2,1)S(1)}, u32[]{:S(2)}, u32[]{:S(2)}) %collective-permute-start.5) | collective-permute-done | bytes 262176 | tf_op jit(solution)/shard_map/ppermute | solution.py:62
  99.7 9.9 %collective-permute-done.6 = bf16[512,256]{1,0:T(8,128)(2,1)S(1)} collective-permute-done((bf16[512,256]{1,0:T(8,128)(2,1)S(1)}, bf16[512,256]{1,0:T(8,128)(2,1)S(1)}, u32[]{:S(2)}, u32[]{:S(2)}) %collective-permute-start.6) | collective-permute-done | bytes 262176 | tf_op jit(solution)/shard_map/ppermute | solution.py:62
  111.6 2.0 gather_fusion.1
  113.6 8.7 %convolution_bitcast_fusion = f32[2048,256]{1,0:T(8,128)S(1)} fusion(bf16[2048,4096]{1,0:T(8,128)(2,1)} %a_ref.1, bf16[4096,256]{1,0:T(8,128)(2,1)} %bitcast.144), kind=kOutput, calls=%fused_computation.16 | convolution fusion | flops 4294967296 | bytes 20971520 | tf_op jit(solution)/shard_map/dot_general | solution.py:17
  124.0 12.6 %collective-permute-done.12 = bf16[1024,256]{1,0:T(8,128)(2,1)S(1)} collective-permute-done((bf16[1024,256]{1,0:T(8,128)(2,1)S(1)}, bf16[1024,256]{1,0:T(8,128)(2,1)S(1)}, u32[]{:S(2)}, u32[]{:S(2)}) %collective-permute-start.12) | collective-permute-done | bytes 524320 | tf_op jit(solution)/shard_map/ppermute | solution.py:37
  139.6 10.6 %collective-permute-done.13 = bf16[1024,256]{1,0:T(8,128)(2,1)S(1)} collective-permute-done((bf16[1024,256]{1,0:T(8,128)(2,1)S(1)}, bf16[1024,256]{1,0:T(8,128)(2,1)S(1)}, u32[]{:S(2)}, u32[]{:S(2)}) %collective-permute-start.13) | collective-permute-done | bytes 524320 | tf_op jit(solution)/shard_map/ppermute | solution.py:37
  151.2 9.4 %shard_map.77 = bf16[2,4,512,256]{3,2,1,0:T(8,128)(2,1)S(1)} custom-call(s32[2]{0:T(128)S(1)} %pad_add_fusion.1.which_ref, bf16[2048,4096]{1,0:T(8,128)(2,1)} %a_ref.1, bf16[2048,256]{1,0:T(8,128)(2,1)S(1)} %pad_maximum_fusion.x_ref), custom_call_target="tpu_custom_call" | custom-call | flops 4294967296 | bytes 16777216 | tf_op jit(solution)/shard_map/pallas_call | solution.py:91
  160.8 2.6 collective-permute-done.16
  163.6 5.5 %collective-permute-start.19 = (bf16[512,256]{1,0:T(8,128)(2,1)S(1)}, bf16[512,256]{1,0:T(8,128)(2,1)S(1)}, u32[]{:S(2)}, u32[]{:S(2)}) collective-permute-start(bf16[512,256]{1,0:T(8,128)(2,1)S(1)} %get-tuple-element.125), channel_id=1, source_target_pairs={{0,6},{2,0},{4,2},{6,4},{1,7},{3,1},{5,3},{7,5},{8,14},{10,8},{12,... | collective-permute-start | bytes 786440 | tf_op jit(solution)/shard_map/ppermute | solution.py:182
  170.1 5.7 %collective-permute-done.19 = bf16[512,256]{1,0:T(8,128)(2,1)S(1)} collective-permute-done((bf16[512,256]{1,0:T(8,128)(2,1)S(1)}, bf16[512,256]{1,0:T(8,128)(2,1)S(1)}, u32[]{:S(2)}, u32[]{:S(2)}) %collective-permute-start.19) | collective-permute-done | bytes 262176 | tf_op jit(solution)/shard_map/ppermute | solution.py:182
  175.8 17.5 %collective-permute-done.18 = bf16[512,256]{1,0:T(8,128)(2,1)S(1)} collective-permute-done((bf16[512,256]{1,0:T(8,128)(2,1)S(1)}, bf16[512,256]{1,0:T(8,128)(2,1)S(1)}, u32[]{:S(2)}, u32[]{:S(2)}) %collective-permute-start.18) | collective-permute-done | bytes 262176 | tf_op jit(solution)/shard_map/ppermute | solution.py:182
  194.3 40.9 %all_to_all.18 = bf16[32,96,256]{2,1,0:T(8,128)(2,1)S(1)} all-to-all(bf16[32,96,256]{2,1,0:T(8,128)(2,1)S(1)} %bitcast.143), channel_id=1, replica_groups=mesh['leaf'=4,'row'=4,'col'=2] {'leaf','row','col'}, dimensions={0} | all-to-all | bytes 3145728 | tf_op jit(solution)/shard_map/all_to_all | solution.py:277
  235.3 1.9 fusion.8
  237.2 9.4 %shard_map.78 = f32[3072,256]{1,0:T(8,128)S(1)} custom-call(bf16[3072,3072]{1,0:T(8,128)(2,1)} %bitcast.140, bf16[3072,256]{1,0:T(8,128)(2,1)S(1)} %bitcast.133), custom_call_target="tpu_custom_call" | custom-call | flops 4831838208 | bytes 18874368 | tf_op jit(solution)/shard_map/pallas_call | solution.py:151
  246.9 3.4 collective-permute-done.20
  251.2 4.0 %shard_map.79 = (bf16[512,256]{1,0:T(8,128)(2,1)S(1)}, bf16[512,256]{1,0:T(8,128)(2,1)S(1)}) custom-call(bf16[3072,6144]{1,0:T(8,128)(2,1)} %bitcast.134, bf16[3072,256]{1,0:T(8,128)(2,1)S(1)} %subtract_convert_fusion.x_ref), custom_call_target="tpu_custom_call" | custom-call | flops 1610612736 | bytes 6291456 | tf_op jit(solution)/shard_map/pallas_call | solution.py:125
  255.4 2.0 collective-permute-start.23
  257.4 4.0 %shard_map.80 = (bf16[512,256]{1,0:T(8,128)(2,1)S(1)}, bf16[512,256]{1,0:T(8,128)(2,1)S(1)}) custom-call(bf16[3072,6144]{1,0:T(8,128)(2,1)} %bitcast.135, bf16[3072,256]{1,0:T(8,128)(2,1)S(1)} %subtract_convert_fusion.x_ref), custom_call_target="tpu_custom_call" | custom-call | flops 1610612736 | bytes 6291456 | tf_op jit(solution)/shard_map/pallas_call | solution.py:125
  261.4 3.1 collective-permute-done.21
  265.9 3.4 collective-permute-done.23
  270.4 4.0 %shard_map.81 = (bf16[512,256]{1,0:T(8,128)(2,1)S(1)}, bf16[512,256]{1,0:T(8,128)(2,1)S(1)}) custom-call(bf16[3072,6144]{1,0:T(8,128)(2,1)} %bitcast.136, bf16[3072,256]{1,0:T(8,128)(2,1)S(1)} %subtract_convert_fusion.x_ref), custom_call_target="tpu_custom_call" | custom-call | flops 1610612736 | bytes 6291456 | tf_op jit(solution)/shard_map/pallas_call | solution.py:125
  274.4 3.0 collective-permute-start.27
  277.8 7.0 %collective-permute-done.27 = bf16[512,256]{1,0:T(8,128)(2,1)S(1)} collective-permute-done((bf16[512,256]{1,0:T(8,128)(2,1)S(1)}, bf16[512,256]{1,0:T(8,128)(2,1)S(1)}, u32[]{:S(2)}, u32[]{:S(2)}) %collective-permute-start.27) | collective-permute-done | bytes 262176 | tf_op jit(solution)/shard_map/ppermute | solution.py:219
  284.8 2.1 collective-permute-start.28
  288.2 4.0 %shard_map.82 = (bf16[512,256]{1,0:T(8,128)(2,1)S(1)}, bf16[512,256]{1,0:T(8,128)(2,1)S(1)}) custom-call(bf16[3072,6144]{1,0:T(8,128)(2,1)} %bitcast.137, bf16[3072,256]{1,0:T(8,128)(2,1)S(1)} %subtract_convert_fusion.x_ref), custom_call_target="tpu_custom_call" | custom-call | flops 1610612736 | bytes 6291456 | tf_op jit(solution)/shard_map/pallas_call | solution.py:125
  292.7 4.6 %collective-permute-start.30 = (bf16[512,256]{1,0:T(8,128)(2,1)S(1)}, bf16[512,256]{1,0:T(8,128)(2,1)S(1)}, u32[]{:S(2)}, u32[]{:S(2)}) collective-permute-start(bf16[512,256]{1,0:T(8,128)(2,1)S(1)} %add_select_fusion.5), channel_id=1, source_target_pairs={{0,2},{2,0},{4,6},{6,4},{1,3},{3,1},{5,7},{7,5},{8,10},{10,8},{12,... | collective-permute-start | bytes 786440 | tf_op jit(solution)/shard_map/ppermute | solution.py:219
  297.5 1.9 collective-permute-start.32
  301.1 4.0 %shard_map.83 = (bf16[512,256]{1,0:T(8,128)(2,1)S(1)}, bf16[512,256]{1,0:T(8,128)(2,1)S(1)}) custom-call(bf16[3072,6144]{1,0:T(8,128)(2,1)} %bitcast.138, bf16[3072,256]{1,0:T(8,128)(2,1)S(1)} %subtract_convert_fusion.x_ref), custom_call_target="tpu_custom_call" | custom-call | flops 1610612736 | bytes 6291456 | tf_op jit(solution)/shard_map/pallas_call | solution.py:125
  305.3 4.8 %collective-permute-start.34 = (bf16[512,256]{1,0:T(8,128)(2,1)S(1)}, bf16[512,256]{1,0:T(8,128)(2,1)S(1)}, u32[]{:S(2)}, u32[]{:S(2)}) collective-permute-start(bf16[512,256]{1,0:T(8,128)(2,1)S(1)} %add_select_fusion.3), channel_id=1, source_target_pairs={{0,2},{2,0},{4,6},{6,4},{1,3},{3,1},{5,7},{7,5},{8,10},{10,8},{12,... | collective-permute-start | bytes 786440 | tf_op jit(solution)/shard_map/ppermute | solution.py:219
  310.2 2.2 collective-permute-start.36
  314.0 4.0 %shard_map.84 = (bf16[512,256]{1,0:T(8,128)(2,1)S(1)}, bf16[512,256]{1,0:T(8,128)(2,1)S(1)}) custom-call(bf16[3072,6144]{1,0:T(8,128)(2,1)} %bitcast.139, bf16[3072,256]{1,0:T(8,128)(2,1)S(1)} %subtract_convert_fusion.x_ref), custom_call_target="tpu_custom_call" | custom-call | flops 1610612736 | bytes 6291456 | tf_op jit(solution)/shard_map/pallas_call | solution.py:125
  318.1 4.6 %collective-permute-start.38 = (bf16[512,256]{1,0:T(8,128)(2,1)S(1)}, bf16[512,256]{1,0:T(8,128)(2,1)S(1)}, u32[]{:S(2)}, u32[]{:S(2)}) collective-permute-start(bf16[512,256]{1,0:T(8,128)(2,1)S(1)} %add_select_fusion.1), channel_id=1, source_target_pairs={{0,2},{2,0},{4,6},{6,4},{1,3},{3,1},{5,7},{7,5},{8,10},{10,8},{12,... | collective-permute-start | bytes 786440 | tf_op jit(solution)/shard_map/ppermute | solution.py:219
  322.9 3.5 collective-permute-start.40
  328.2 6.7 %collective-permute-start.42 = (bf16[512,256]{1,0:T(8,128)(2,1)S(1)}, bf16[512,256]{1,0:T(8,128)(2,1)S(1)}, u32[]{:S(2)}, u32[]{:S(2)}) collective-permute-start(bf16[512,256]{1,0:T(8,128)(2,1)S(1)} %add.310), channel_id=1, source_target_pairs={{0,2},{2,0},{4,6},{6,4},{1,3},{3,1},{5,7},{7,5},{8,10},{10,8},{12,... | collective-permute-start | bytes 786440 | tf_op jit(solution)/shard_map/ppermute | solution.py:219
  335.0 5.1 %collective-permute-start.44 = (bf16[512,256]{1,0:T(8,128)(2,1)S(1)}, bf16[512,256]{1,0:T(8,128)(2,1)S(1)}, u32[]{:S(2)}, u32[]{:S(2)}) collective-permute-start(bf16[512,256]{1,0:T(8,128)(2,1)S(1)} %add.314), channel_id=1, source_target_pairs={{0,2},{2,0},{4,6},{6,4},{1,3},{3,1},{5,7},{7,5},{8,10},{10,8},{12,... | collective-permute-start | bytes 786440 | tf_op jit(solution)/shard_map/ppermute | solution.py:219
  341.9 6.7 %collective-permute-start.46 = (bf16[512,256]{1,0:T(8,128)(2,1)S(1)}, bf16[512,256]{1,0:T(8,128)(2,1)S(1)}, u32[]{:S(2)}, u32[]{:S(2)}) collective-permute-start(bf16[512,256]{1,0:T(8,128)(2,1)S(1)} %add.318), channel_id=1, source_target_pairs={{0,2},{2,0},{4,6},{6,4},{1,3},{3,1},{5,7},{7,5},{8,10},{10,8},{12,... | collective-permute-start | bytes 786440 | tf_op jit(solution)/shard_map/ppermute | solution.py:219
  348.6 3.3 collective-permute-start.48
  353.0 3.2 collective-permute-done.48
  (169 shorter events, 37.7 us)
Async XLA Ops:
  21.0 4.1 %collective-permute-start = (bf16[3072,256]{1,0:T(8,128)(2,1)}, bf16[3072,256]{1,0:T(8,128)(2,1)S(1)}, u32[]{:S(2)}, u32[]{:S(2)}) collective-permute-start(bf16[3072,256]{1,0:T(8,128)(2,1)} %get-tuple-element.131), channel_id=1, source_target_pairs={{0,1},{1,0},{2,3},{3,2},{4,5},{5,4},{6,7},{7,6},{8,9},{9,8},{10,11... | collective-permute-start | bytes 4718600 | tf_op jit(solution)/shard_map/ppermute | solution.py:26
  41.7 45.8 %all-to-all-start = ((bf16[32,96,256]{2,1,0:T(8,128)(2,1)}), bf16[32,96,256]{2,1,0:T(8,128)(2,1)S(1)}, u32[]{:S(2)}, u32[]{:S(2)}) async-start(bf16[32,96,256]{2,1,0:T(8,128)(2,1)} %bitcast.16), calls=%async_computation | async-start | bytes 3145728 | tf_op jit(solution)/shard_map/all_to_all | solution.py:264
  50.6 10.3 %collective-permute-start.3 = (s32[32,96]{1,0:T(8,128)S(1)}, s32[32,96]{1,0:T(8,128)S(1)}, u32[]{:S(2)}, u32[]{:S(2)}) collective-permute-start(s32[32,96]{1,0:T(8,128)S(1)} %reshape.275), channel_id=1, source_target_pairs={{0,24},{8,16},{16,8},{24,0},{1,25},{9,17},{17,9},{25,1},{2,26},{10... | collective-permute-start | bytes 36872 | tf_op jit(solution)/shard_map/ppermute | solution.py:47
  53.3 7.6 %collective-permute-start.2 = (s32[32,96]{1,0:T(8,128)S(1)}, s32[32,96]{1,0:T(8,128)S(1)}, u32[]{:S(2)}, u32[]{:S(2)}) collective-permute-start(s32[32,96]{1,0:T(8,128)S(1)} %reshape.275), channel_id=1, source_target_pairs={{0,16},{8,24},{16,0},{24,8},{1,17},{9,25},{17,1},{25,9},{2,18},{10... | collective-permute-start | bytes 36872 | tf_op jit(solution)/shard_map/ppermute | solution.py:47
  53.9 7.0 %collective-permute-start.1 = (s32[32,96]{1,0:T(8,128)S(1)}, s32[32,96]{1,0:T(8,128)S(1)}, u32[]{:S(2)}, u32[]{:S(2)}) collective-permute-start(s32[32,96]{1,0:T(8,128)S(1)} %reshape.275), channel_id=1, source_target_pairs={{0,8},{8,0},{16,24},{24,16},{1,9},{9,1},{17,25},{25,17},{2,10},{10... | collective-permute-start | bytes 36872 | tf_op jit(solution)/shard_map/ppermute | solution.py:47
  88.3 11.3 %collective-permute-start.5 = (bf16[512,256]{1,0:T(8,128)(2,1)S(1)}, bf16[512,256]{1,0:T(8,128)(2,1)S(1)}, u32[]{:S(2)}, u32[]{:S(2)}) collective-permute-start(bf16[512,256]{1,0:T(8,128)(2,1)S(1)} %get-tuple-element.134), channel_id=1, source_target_pairs={{0,2},{2,4},{4,6},{6,0},{1,3},{3,5},{5,7},{7,1},{8,10},{10,12},{12... | collective-permute-start | bytes 786440 | tf_op jit(solution)/shard_map/ppermute | solution.py:62
  88.6 21.0 %collective-permute-start.6 = (bf16[512,256]{1,0:T(8,128)(2,1)S(1)}, bf16[512,256]{1,0:T(8,128)(2,1)S(1)}, u32[]{:S(2)}, u32[]{:S(2)}) collective-permute-start(bf16[512,256]{1,0:T(8,128)(2,1)S(1)} %get-tuple-element.134), channel_id=1, source_target_pairs={{0,4},{2,6},{4,0},{6,2},{1,5},{3,7},{5,1},{7,3},{8,12},{10,14},{12... | collective-permute-start | bytes 786440 | tf_op jit(solution)/shard_map/ppermute | solution.py:62
  89.0 20.7 %collective-permute-start.7 = (bf16[512,256]{1,0:T(8,128)(2,1)S(1)}, bf16[512,256]{1,0:T(8,128)(2,1)S(1)}, u32[]{:S(2)}, u32[]{:S(2)}) collective-permute-start(bf16[512,256]{1,0:T(8,128)(2,1)S(1)} %get-tuple-element.134), channel_id=1, source_target_pairs={{0,6},{2,0},{4,2},{6,4},{1,7},{3,1},{5,3},{7,5},{8,14},{10,8},{12,... | collective-permute-start | bytes 786440 | tf_op jit(solution)/shard_map/ppermute | solution.py:62
  92.5 17.7 %collective-permute-start.8 = (bf16[512,256]{1,0:T(8,128)(2,1)S(1)}, bf16[512,256]{1,0:T(8,128)(2,1)S(1)}, u32[]{:S(2)}, u32[]{:S(2)}) collective-permute-start(bf16[512,256]{1,0:T(8,128)(2,1)S(1)} %get-tuple-element.134), channel_id=1, source_target_pairs={{0,1},{1,0},{2,3},{3,2},{4,5},{5,4},{6,7},{7,6},{8,9},{9,8},{10,11... | collective-permute-start | bytes 786440 | tf_op jit(solution)/shard_map/ppermute | solution.py:68
  99.7 10.6 %collective-permute-start.9 = (bf16[512,256]{1,0:T(8,128)(2,1)S(1)}, bf16[512,256]{1,0:T(8,128)(2,1)S(1)}, u32[]{:S(2)}, u32[]{:S(2)}) collective-permute-start(bf16[512,256]{1,0:T(8,128)(2,1)S(1)} %collective-permute-done.5), channel_id=1, source_target_pairs={{0,1},{1,0},{2,3},{3,2},{4,5},{5,4},{6,7},{7,6},{8,9},{9,8},{10,11... | collective-permute-start | bytes 786440 | tf_op jit(solution)/shard_map/ppermute | solution.py:68
  109.7 1.9 collective-permute-start.11
  122.4 14.1 %collective-permute-start.12 = (bf16[1024,256]{1,0:T(8,128)(2,1)S(1)}, bf16[1024,256]{1,0:T(8,128)(2,1)S(1)}, u32[]{:S(2)}, u32[]{:S(2)}) collective-permute-start(bf16[1024,256]{1,0:T(8,128)(2,1)S(1)} %get-tuple-element.122), channel_id=1, source_target_pairs={{0,8},{8,0},{16,24},{24,16},{1,9},{9,1},{17,25},{25,17},{2,10},{10... | collective-permute-start | bytes 1572872 | tf_op jit(solution)/shard_map/ppermute | solution.py:37
  122.9 13.8 %collective-permute-start.14 = (bf16[1024,256]{1,0:T(8,128)(2,1)S(1)}, bf16[1024,256]{1,0:T(8,128)(2,1)S(1)}, u32[]{:S(2)}, u32[]{:S(2)}) collective-permute-start(bf16[1024,256]{1,0:T(8,128)(2,1)S(1)} %get-tuple-element.123), channel_id=1, source_target_pairs={{0,16},{8,24},{16,0},{24,8},{1,17},{9,25},{17,1},{25,9},{2,18},{10... | collective-permute-start | bytes 1572872 | tf_op jit(solution)/shard_map/ppermute | solution.py:37
  137.0 13.2 %collective-permute-start.13 = (bf16[1024,256]{1,0:T(8,128)(2,1)S(1)}, bf16[1024,256]{1,0:T(8,128)(2,1)S(1)}, u32[]{:S(2)}, u32[]{:S(2)}) collective-permute-start(bf16[1024,256]{1,0:T(8,128)(2,1)S(1)} %get-tuple-element.120), channel_id=1, source_target_pairs={{0,16},{8,24},{16,0},{24,8},{1,17},{9,25},{17,1},{25,9},{2,18},{10... | collective-permute-start | bytes 1572872 | tf_op jit(solution)/shard_map/ppermute | solution.py:37
  138.1 12.7 %collective-permute-start.15 = (bf16[1024,256]{1,0:T(8,128)(2,1)S(1)}, bf16[1024,256]{1,0:T(8,128)(2,1)S(1)}, u32[]{:S(2)}, u32[]{:S(2)}) collective-permute-start(bf16[1024,256]{1,0:T(8,128)(2,1)S(1)} %get-tuple-element.121), channel_id=1, source_target_pairs={{0,8},{8,0},{16,24},{24,16},{1,9},{9,1},{17,25},{25,17},{2,10},{10... | collective-permute-start | bytes 1572872 | tf_op jit(solution)/shard_map/ppermute | solution.py:37
  160.7 2.7 collective-permute-start.16
  163.6 12.2 %collective-permute-start.19 = (bf16[512,256]{1,0:T(8,128)(2,1)S(1)}, bf16[512,256]{1,0:T(8,128)(2,1)S(1)}, u32[]{:S(2)}, u32[]{:S(2)}) collective-permute-start(bf16[512,256]{1,0:T(8,128)(2,1)S(1)} %get-tuple-element.125), channel_id=1, source_target_pairs={{0,6},{2,0},{4,2},{6,4},{1,7},{3,1},{5,3},{7,5},{8,14},{10,8},{12,... | collective-permute-start | bytes 786440 | tf_op jit(solution)/shard_map/ppermute | solution.py:182
  169.1 24.3 %collective-permute-start.18 = (bf16[512,256]{1,0:T(8,128)(2,1)S(1)}, bf16[512,256]{1,0:T(8,128)(2,1)S(1)}, u32[]{:S(2)}, u32[]{:S(2)}) collective-permute-start(bf16[512,256]{1,0:T(8,128)(2,1)S(1)} %get-tuple-element.126), channel_id=1, source_target_pairs={{0,4},{2,6},{4,0},{6,2},{1,5},{3,7},{5,1},{7,3},{8,12},{10,14},{12... | collective-permute-start | bytes 786440 | tf_op jit(solution)/shard_map/ppermute | solution.py:182
  170.1 23.2 %collective-permute-start.17 = (bf16[512,256]{1,0:T(8,128)(2,1)S(1)}, bf16[512,256]{1,0:T(8,128)(2,1)S(1)}, u32[]{:S(2)}, u32[]{:S(2)}) collective-permute-start(bf16[512,256]{1,0:T(8,128)(2,1)S(1)} %get-tuple-element.124), channel_id=1, source_target_pairs={{0,2},{2,4},{4,6},{6,0},{1,3},{3,5},{5,7},{7,1},{8,10},{10,12},{12... | collective-permute-start | bytes 786440 | tf_op jit(solution)/shard_map/ppermute | solution.py:182
  246.8 3.5 collective-permute-start.20
  255.3 9.2 %collective-permute-start.21 = (bf16[512,256]{1,0:T(8,128)(2,1)S(1)}, bf16[512,256]{1,0:T(8,128)(2,1)S(1)}, u32[]{:S(2)}, u32[]{:S(2)}) collective-permute-start(bf16[512,256]{1,0:T(8,128)(2,1)S(1)} %get-tuple-element.60), channel_id=1, source_target_pairs={{0,2},{2,0},{4,6},{6,4},{1,3},{3,1},{5,7},{7,5},{8,10},{10,8},{12,... | collective-permute-start | bytes 786440 | tf_op jit(solution)/shard_map/ppermute | solution.py:219
  255.4 14.0 %collective-permute-start.23 = (bf16[512,256]{1,0:T(8,128)(2,1)S(1)}, bf16[512,256]{1,0:T(8,128)(2,1)S(1)}, u32[]{:S(2)}, u32[]{:S(2)}) collective-permute-start(bf16[512,256]{1,0:T(8,128)(2,1)S(1)} %get-tuple-element.67), channel_id=1, source_target_pairs={{0,2},{2,0},{4,6},{6,4},{1,3},{3,1},{5,7},{7,5},{8,10},{10,8},{12,... | collective-permute-start | bytes 786440 | tf_op jit(solution)/shard_map/ppermute | solution.py:219
  265.3 12.2 %collective-permute-start.22 = (bf16[512,256]{1,0:T(8,128)(2,1)}, bf16[512,256]{1,0:T(8,128)(2,1)S(1)}, u32[]{:S(2)}, u32[]{:S(2)}) collective-permute-start(bf16[512,256]{1,0:T(8,128)(2,1)} %add.275), channel_id=1, source_target_pairs={{2,4},{4,2},{3,5},{5,3},{10,12},{12,10},{11,13},{13,11},{18,20},{2... | collective-permute-start | bytes 786440 | tf_op jit(solution)/shard_map/ppermute | solution.py:215
  269.4 8.2 %collective-permute-start.24 = (bf16[512,256]{1,0:T(8,128)(2,1)S(1)}, bf16[512,256]{1,0:T(8,128)(2,1)S(1)}, u32[]{:S(2)}, u32[]{:S(2)}) collective-permute-start(bf16[512,256]{1,0:T(8,128)(2,1)S(1)} %get-tuple-element.71), channel_id=1, source_target_pairs={{0,2},{2,0},{4,6},{6,4},{1,3},{3,1},{5,7},{7,5},{8,10},{10,8},{12,... | collective-permute-start | bytes 786440 | tf_op jit(solution)/shard_map/ppermute | solution.py:219
  269.7 8.0 %collective-permute-start.26 = (bf16[512,256]{1,0:T(8,128)(2,1)S(1)}, bf16[512,256]{1,0:T(8,128)(2,1)S(1)}, u32[]{:S(2)}, u32[]{:S(2)}) collective-permute-start(bf16[512,256]{1,0:T(8,128)(2,1)S(1)} %add.278), channel_id=1, source_target_pairs={{2,4},{4,2},{3,5},{5,3},{10,12},{12,10},{11,13},{13,11},{18,20},{2... | collective-permute-start | bytes 786440 | tf_op jit(solution)/shard_map/ppermute | solution.py:215
  274.4 10.3 %collective-permute-start.27 = (bf16[512,256]{1,0:T(8,128)(2,1)S(1)}, bf16[512,256]{1,0:T(8,128)(2,1)S(1)}, u32[]{:S(2)}, u32[]{:S(2)}) collective-permute-start(bf16[512,256]{1,0:T(8,128)(2,1)S(1)} %get-tuple-element.76), channel_id=1, source_target_pairs={{0,2},{2,0},{4,6},{6,4},{1,3},{3,1},{5,7},{7,5},{8,10},{10,8},{12,... | collective-permute-start | bytes 786440 | tf_op jit(solution)/shard_map/ppermute | solution.py:219
  277.6 14.6 %collective-permute-start.25 = (bf16[512,256]{1,0:T(8,128)(2,1)S(1)}, bf16[512,256]{1,0:T(8,128)(2,1)S(1)}, u32[]{:S(2)}, u32[]{:S(2)}) collective-permute-start(bf16[512,256]{1,0:T(8,128)(2,1)S(1)} %add_select_fusion.7), channel_id=1, source_target_pairs={{0,2},{2,0},{4,6},{6,4},{1,3},{3,1},{5,7},{7,5},{8,10},{10,8},{12,... | collective-permute-start | bytes 786440 | tf_op jit(solution)/shard_map/ppermute | solution.py:219
  284.8 12.6 %collective-permute-start.28 = (bf16[512,256]{1,0:T(8,128)(2,1)S(1)}, bf16[512,256]{1,0:T(8,128)(2,1)S(1)}, u32[]{:S(2)}, u32[]{:S(2)}) collective-permute-start(bf16[512,256]{1,0:T(8,128)(2,1)S(1)} %add_select_fusion.6), channel_id=1, source_target_pairs={{0,2},{2,0},{4,6},{6,4},{1,3},{3,1},{5,7},{7,5},{8,10},{10,8},{12,... | collective-permute-start | bytes 786440 | tf_op jit(solution)/shard_map/ppermute | solution.py:219
  286.9 5.8 %collective-permute-start.29 = (bf16[512,256]{1,0:T(8,128)(2,1)S(1)}, bf16[512,256]{1,0:T(8,128)(2,1)S(1)}, u32[]{:S(2)}, u32[]{:S(2)}) collective-permute-start(bf16[512,256]{1,0:T(8,128)(2,1)S(1)} %add.279), channel_id=1, source_target_pairs={{2,4},{4,2},{3,5},{5,3},{10,12},{12,10},{11,13},{13,11},{18,20},{2... | collective-permute-start | bytes 786440 | tf_op jit(solution)/shard_map/ppermute | solution.py:215
  287.5 9.9 %collective-permute-start.31 = (bf16[512,256]{1,0:T(8,128)(2,1)S(1)}, bf16[512,256]{1,0:T(8,128)(2,1)S(1)}, u32[]{:S(2)}, u32[]{:S(2)}) collective-permute-start(bf16[512,256]{1,0:T(8,128)(2,1)S(1)} %add.283), channel_id=1, source_target_pairs={{2,4},{4,2},{3,5},{5,3},{10,12},{12,10},{11,13},{13,11},{18,20},{2... | collective-permute-start | bytes 786440 | tf_op jit(solution)/shard_map/ppermute | solution.py:215
  292.7 12.4 %collective-permute-start.30 = (bf16[512,256]{1,0:T(8,128)(2,1)S(1)}, bf16[512,256]{1,0:T(8,128)(2,1)S(1)}, u32[]{:S(2)}, u32[]{:S(2)}) collective-permute-start(bf16[512,256]{1,0:T(8,128)(2,1)S(1)} %add_select_fusion.5), channel_id=1, source_target_pairs={{0,2},{2,0},{4,6},{6,4},{1,3},{3,1},{5,7},{7,5},{8,10},{10,8},{12,... | collective-permute-start | bytes 786440 | tf_op jit(solution)/shard_map/ppermute | solution.py:219
  297.5 12.6 %collective-permute-start.32 = (bf16[512,256]{1,0:T(8,128)(2,1)S(1)}, bf16[512,256]{1,0:T(8,128)(2,1)S(1)}, u32[]{:S(2)}, u32[]{:S(2)}) collective-permute-start(bf16[512,256]{1,0:T(8,128)(2,1)S(1)} %add_select_fusion.4), channel_id=1, source_target_pairs={{0,2},{2,0},{4,6},{6,4},{1,3},{3,1},{5,7},{7,5},{8,10},{10,8},{12,... | collective-permute-start | bytes 786440 | tf_op jit(solution)/shard_map/ppermute | solution.py:219
  299.4 5.9 %collective-permute-start.33 = (bf16[512,256]{1,0:T(8,128)(2,1)S(1)}, bf16[512,256]{1,0:T(8,128)(2,1)S(1)}, u32[]{:S(2)}, u32[]{:S(2)}) collective-permute-start(bf16[512,256]{1,0:T(8,128)(2,1)S(1)} %add.287), channel_id=1, source_target_pairs={{2,4},{4,2},{3,5},{5,3},{10,12},{12,10},{11,13},{13,11},{18,20},{2... | collective-permute-start | bytes 786440 | tf_op jit(solution)/shard_map/ppermute | solution.py:215
  300.0 10.1 %collective-permute-start.35 = (bf16[512,256]{1,0:T(8,128)(2,1)S(1)}, bf16[512,256]{1,0:T(8,128)(2,1)S(1)}, u32[]{:S(2)}, u32[]{:S(2)}) collective-permute-start(bf16[512,256]{1,0:T(8,128)(2,1)S(1)} %add.291), channel_id=1, source_target_pairs={{2,4},{4,2},{3,5},{5,3},{10,12},{12,10},{11,13},{13,11},{18,20},{2... | collective-permute-start | bytes 786440 | tf_op jit(solution)/shard_map/ppermute | solution.py:215
  305.3 12.7 %collective-permute-start.34 = (bf16[512,256]{1,0:T(8,128)(2,1)S(1)}, bf16[512,256]{1,0:T(8,128)(2,1)S(1)}, u32[]{:S(2)}, u32[]{:S(2)}) collective-permute-start(bf16[512,256]{1,0:T(8,128)(2,1)S(1)} %add_select_fusion.3), channel_id=1, source_target_pairs={{0,2},{2,0},{4,6},{6,4},{1,3},{3,1},{5,7},{7,5},{8,10},{10,8},{12,... | collective-permute-start | bytes 786440 | tf_op jit(solution)/shard_map/ppermute | solution.py:219
  310.2 12.6 %collective-permute-start.36 = (bf16[512,256]{1,0:T(8,128)(2,1)S(1)}, bf16[512,256]{1,0:T(8,128)(2,1)S(1)}, u32[]{:S(2)}, u32[]{:S(2)}) collective-permute-start(bf16[512,256]{1,0:T(8,128)(2,1)S(1)} %add_select_fusion.2), channel_id=1, source_target_pairs={{0,2},{2,0},{4,6},{6,4},{1,3},{3,1},{5,7},{7,5},{8,10},{10,8},{12,... | collective-permute-start | bytes 786440 | tf_op jit(solution)/shard_map/ppermute | solution.py:219
  312.3 5.8 %collective-permute-start.37 = (bf16[512,256]{1,0:T(8,128)(2,1)S(1)}, bf16[512,256]{1,0:T(8,128)(2,1)S(1)}, u32[]{:S(2)}, u32[]{:S(2)}) collective-permute-start(bf16[512,256]{1,0:T(8,128)(2,1)S(1)} %add.295), channel_id=1, source_target_pairs={{2,4},{4,2},{3,5},{5,3},{10,12},{12,10},{11,13},{13,11},{18,20},{2... | collective-permute-start | bytes 786440 | tf_op jit(solution)/shard_map/ppermute | solution.py:215
  313.0 9.8 %collective-permute-start.39 = (bf16[512,256]{1,0:T(8,128)(2,1)S(1)}, bf16[512,256]{1,0:T(8,128)(2,1)S(1)}, u32[]{:S(2)}, u32[]{:S(2)}) collective-permute-start(bf16[512,256]{1,0:T(8,128)(2,1)S(1)} %add.299), channel_id=1, source_target_pairs={{2,4},{4,2},{3,5},{5,3},{10,12},{12,10},{11,13},{13,11},{18,20},{2... | collective-permute-start | bytes 786440 | tf_op jit(solution)/shard_map/ppermute | solution.py:215
  318.1 9.9 %collective-permute-start.38 = (bf16[512,256]{1,0:T(8,128)(2,1)S(1)}, bf16[512,256]{1,0:T(8,128)(2,1)S(1)}, u32[]{:S(2)}, u32[]{:S(2)}) collective-permute-start(bf16[512,256]{1,0:T(8,128)(2,1)S(1)} %add_select_fusion.1), channel_id=1, source_target_pairs={{0,2},{2,0},{4,6},{6,4},{1,3},{3,1},{5,7},{7,5},{8,10},{10,8},{12,... | collective-permute-start | bytes 786440 | tf_op jit(solution)/shard_map/ppermute | solution.py:219
  322.9 12.1 %collective-permute-start.40 = (bf16[512,256]{1,0:T(8,128)(2,1)S(1)}, bf16[512,256]{1,0:T(8,128)(2,1)S(1)}, u32[]{:S(2)}, u32[]{:S(2)}) collective-permute-start(bf16[512,256]{1,0:T(8,128)(2,1)S(1)} %add_select_fusion), channel_id=1, source_target_pairs={{0,2},{2,0},{4,6},{6,4},{1,3},{3,1},{5,7},{7,5},{8,10},{10,8},{12,... | collective-permute-start | bytes 786440 | tf_op jit(solution)/shard_map/ppermute | solution.py:219
  326.4 1.6 collective-permute-start.41
  327.0 7.8 %collective-permute-start.43 = (bf16[512,256]{1,0:T(8,128)(2,1)S(1)}, bf16[512,256]{1,0:T(8,128)(2,1)S(1)}, u32[]{:S(2)}, u32[]{:S(2)}) collective-permute-start(bf16[512,256]{1,0:T(8,128)(2,1)S(1)} %add.307), channel_id=1, source_target_pairs={{2,4},{4,2},{3,5},{5,3},{10,12},{12,10},{11,13},{13,11},{18,20},{2... | collective-permute-start | bytes 786440 | tf_op jit(solution)/shard_map/ppermute | solution.py:215
  328.2 23.8 %collective-permute-start.42 = (bf16[512,256]{1,0:T(8,128)(2,1)S(1)}, bf16[512,256]{1,0:T(8,128)(2,1)S(1)}, u32[]{:S(2)}, u32[]{:S(2)}) collective-permute-start(bf16[512,256]{1,0:T(8,128)(2,1)S(1)} %add.310), channel_id=1, source_target_pairs={{0,2},{2,0},{4,6},{6,4},{1,3},{3,1},{5,7},{7,5},{8,10},{10,8},{12,... | collective-permute-start | bytes 786440 | tf_op jit(solution)/shard_map/ppermute | solution.py:219
  335.0 17.0 %collective-permute-start.44 = (bf16[512,256]{1,0:T(8,128)(2,1)S(1)}, bf16[512,256]{1,0:T(8,128)(2,1)S(1)}, u32[]{:S(2)}, u32[]{:S(2)}) collective-permute-start(bf16[512,256]{1,0:T(8,128)(2,1)S(1)} %add.314), channel_id=1, source_target_pairs={{0,2},{2,0},{4,6},{6,4},{1,3},{3,1},{5,7},{7,5},{8,10},{10,8},{12,... | collective-permute-start | bytes 786440 | tf_op jit(solution)/shard_map/ppermute | solution.py:219
  340.2 1.6 collective-permute-start.45
  340.8 7.7 %collective-permute-start.47 = (bf16[512,256]{1,0:T(8,128)(2,1)S(1)}, bf16[512,256]{1,0:T(8,128)(2,1)S(1)}, u32[]{:S(2)}, u32[]{:S(2)}) collective-permute-start(bf16[512,256]{1,0:T(8,128)(2,1)S(1)} %add.315), channel_id=1, source_target_pairs={{2,4},{4,2},{3,5},{5,3},{10,12},{12,10},{11,13},{13,11},{18,20},{2... | collective-permute-start | bytes 786440 | tf_op jit(solution)/shard_map/ppermute | solution.py:215
  341.9 11.0 %collective-permute-start.46 = (bf16[512,256]{1,0:T(8,128)(2,1)S(1)}, bf16[512,256]{1,0:T(8,128)(2,1)S(1)}, u32[]{:S(2)}, u32[]{:S(2)}) collective-permute-start(bf16[512,256]{1,0:T(8,128)(2,1)S(1)} %add.318), channel_id=1, source_target_pairs={{0,2},{2,0},{4,6},{6,4},{1,3},{3,1},{5,7},{7,5},{8,10},{10,8},{12,... | collective-permute-start | bytes 786440 | tf_op jit(solution)/shard_map/ppermute | solution.py:219
  348.6 7.6 %collective-permute-start.48 = (bf16[512,256]{1,0:T(8,128)(2,1)S(1)}, bf16[512,256]{1,0:T(8,128)(2,1)S(1)}, u32[]{:S(2)}, u32[]{:S(2)}) collective-permute-start(bf16[512,256]{1,0:T(8,128)(2,1)S(1)} %add.321), channel_id=1, source_target_pairs={{0,2},{2,0},{4,6},{6,4},{1,3},{3,1},{5,7},{7,5},{8,10},{10,8},{12,... | collective-permute-start | bytes 786440 | tf_op jit(solution)/shard_map/ppermute | solution.py:219
  (11 other events, 92.6 us)
where the time goes:
time: 359 us; the launch traced here: 358 us
  waiting for transfers between devices  121 us (34%)
  starting transfers between devices  85.7 us (24%)
  matrix products  43.4 us (12%)
  Pallas kernels  43 us (12%)
  blocking collectives  40.9 us (11%)
  local copies, waits for them, and re-layouts  11.2 us (3%)
  other arithmetic  11.1 us (3%)
    ppermute x16, starting transfers between devices, solve_and_sum_rows(): outer_got.append(lax.ppermute(send, 'row', ends))  50.9 us
    all_to_all x1, blocking collectives, per_device(): lax.all_to_all(wanted.reshape(devices * per_owner, width), ALL, 0, 0, til...  40.9 us
    dot_general x4, matrix products, matmul(): return jnp.dot(a, x, preferred_element_type=F32)  37.5 us
    all_to_all x1, waiting for transfers between devices, per_device(): arrived = lax.all_to_all(packed, ALL, 0, 0, tiled=True)  24.6 us
    pallas_call x6, Pallas kernels, dot_t(): pl.pallas_call(kernel, grid=(count,), in_specs=[pl.BlockSpec((k, tile), l...  24.1 us
    ppermute x4, waiting for transfers between devices, swap_leaves(): lax.ppermute(h.astype(BF16), 'leaf', [(i, i ^ order[step]) for i in range...  23.9 us
    ppermute x3, waiting for transfers between devices, scatter_rows(): lax.ppermute(summed[d], 'row', [(i, (i + d) % depth) for i in range(depth)])  23.2 us
    ppermute x16, waiting for transfers between devices, solve_and_sum_rows(): outer_got.append(lax.ppermute(send, 'row', ends))  17.4 us
  transfers between devices with their start and end apart: 50, of which 20 were waited for; matrix products, arithmetic and copies ran while one was open for 3% of the time, Pallas kernels for 6%

commit v1 on v0

--- a/solution.py
+++ b/solution.py
@@ -9,8 +9,9 @@
 F32 = jnp.float32
 BF16 = jnp.bfloat16
 CHUNKS = 12
-GROUP = 2
+GROUPS = (1, 1, 2, 2, 2, 2, 2)
 VMEM = 40 * 2**20
+RESIDENT = 8 * 2**20
 
 
 def matmul(a, x):
@@ -23,9 +24,9 @@
 
 def sum_cores(part):
     if lax.axis_size("col") == 2:
-        other = lax.ppermute(part.astype(BF16), "col", [(0, 1), (1, 0)])
-        return part + other.astype(F32)
-    return lax.psum(part, "col")
+        other = lax.ppermute(part, "col", [(0, 1), (1, 0)])
+        return part.astype(F32) + other.astype(F32)
+    return lax.psum(part.astype(F32), "col")
 
 
 def swap_leaves(halves, steps):
@@ -55,25 +56,147 @@
     return lax.all_gather(lists, "col", axis=1)
 
 
-def gather_block(own):
+def matmul_streamed(a, x, dtype):
+    m, k = a.shape
+    width = x.shape[1]
+    tile = m // 6 if m % 96 == 0 else m
+    count = m // tile
+    slots = min(3, count)
+
+    x = pltpu.with_memory_space_constraint(x, pltpu.HBM)
+
+    def kernel(a_ref, x_ref, out_ref, held, x_held, sems, x_sem):
+        def copy(t, slot):
+            rows = pl.ds(pl.multiple_of(t * tile, tile), tile)
+            return pltpu.make_async_copy(a_ref.at[rows, :], held.at[slot], sems.at[slot])
+
+        x_copy = pltpu.make_async_copy(x_ref, x_held, x_sem)
+        x_copy.start()
+        for t in range(slots):
+            copy(t, t).start()
+        x_copy.wait()
+
+        @pl.loop(0, count)
+        def _(t):
+            slot = lax.rem(t, slots)
+            copy(t, slot).wait()
+            rows = pl.ds(pl.multiple_of(t * tile, tile), tile)
+            out_ref[rows, :] = matmul(held[slot], x_held[...]).astype(dtype)
+
+            @pl.when(t + slots < count)
+            def _():
+                copy(t + slots, slot).start()
+
+    return pl.pallas_call(
+        kernel,
+        in_specs=[pl.BlockSpec(memory_space=pltpu.HBM)] * 2,
+        out_specs=pl.BlockSpec(memory_space=pltpu.VMEM),
+        out_shape=jax.ShapeDtypeStruct((m, width), dtype),
+        scratch_shapes=[
+            pltpu.VMEM((slots, tile, k), BF16),
+            pltpu.VMEM((k, width), BF16),
+            pltpu.SemaphoreType.DMA((slots,)),
+            pltpu.SemaphoreType.DMA,
+        ],
+        compiler_params=pltpu.CompilerParams(vmem_limit_bytes=VMEM),
+        cost_estimate=pl.CostEstimate(
+            flops=2 * m * k * width, bytes_accessed=2 * m * k, transcendentals=0
+        ),
+    )(a, x)
+
+
+def add_columns(a, parts, chunks, total):
+    m, k = a.shape
+    rows, width = parts[0].shape
+    count = len(parts)
+    tile = min(m, 512)
+
+    def kernel(chunks_ref, a_ref, *refs):
+        out_ref = refs[-1]
+
+        @pl.loop(0, m // tile)
+        def _(i):
+            at = pl.ds(pl.multiple_of(i * tile, tile), tile)
+            acc = jnp.zeros((tile, width), F32) if total is None else refs[count][at, :]
+            for j in range(count):
+                cols = pl.ds(pl.multiple_of(chunks_ref[j] * rows, rows), rows)
+                acc = acc + matmul(a_ref[at, cols], refs[j][...])
+            out_ref[at, :] = acc
+
+    extra = [] if total is None else [total]
+    return pl.pallas_call(
+        kernel,
+        in_specs=[pl.BlockSpec(memory_space=pltpu.SMEM)]
+        + [pl.BlockSpec(memory_space=pltpu.VMEM)] * (1 + count + len(extra)),
+        out_specs=pl.BlockSpec(memory_space=pltpu.VMEM),
+        out_shape=jax.ShapeDtypeStruct((m, width), F32),
+        compiler_params=pltpu.CompilerParams(vmem_limit_bytes=RESIDENT),
+        cost_estimate=pl.CostEstimate(
+            flops=2 * m * rows * count * width, bytes_accessed=0, transcendentals=0
+        ),
+    )(jnp.stack(chunks).astype(jnp.int32), a, *parts, *extra)
+
+
+def first_columns(a, parts, chunks):
+    m, k = a.shape
+    rows, width = parts[0].shape
+    count = len(parts)
+
+    def kernel(chunks_ref, a_ref, *refs):
+        out_ref = refs[-1]
+        for j in range(count):
+
+            @pl.when(pl.program_id(0) == j)
+            def _():
+                part = matmul(a_ref[...], refs[j][...])
+                out_ref[...] = part if j == 0 else part + out_ref[...]
+
+    return pl.pallas_call(
+        kernel,
+        grid_spec=pltpu.PrefetchScalarGridSpec(
+            num_scalar_prefetch=1,
+            grid=(count,),
+            in_specs=[pl.BlockSpec((m, rows), lambda i, chunks_ref: (0, chunks_ref[i]))]
+            + [pl.BlockSpec((rows, width), lambda i, chunks_ref: (0, 0))] * count,
+            out_specs=pl.BlockSpec((m, width), lambda i, chunks_ref: (0, 0)),
+        ),
+        out_shape=jax.ShapeDtypeStruct((m, width), F32),
+        compiler_params=pltpu.CompilerParams(vmem_limit_bytes=VMEM),
+        cost_estimate=pl.CostEstimate(
+            flops=2 * m * rows * count * width,
+            bytes_accessed=4 * m * rows * count,
+            transcendentals=0,
+        ),
+    )(jnp.stack(chunks).astype(jnp.int32), a, *parts)
+
+
+def gather_and_solve(a, own):
     depth = lax.axis_size("row")
+    cores = lax.axis_size("col")
     z = lax.axis_index("row")
-    parts = [own] + [
+    c = lax.axis_index("col")
+    rows = [own] + [
         lax.ppermute(own, "row", [(i, (i + d) % depth) for i in range(depth)])
         for d in range(1, depth)
     ]
-    cores = lax.axis_size("col")
-    if cores == 2:
-        c = lax.axis_index("col")
-        parts += [lax.ppermute(part, "col", [(0, 1), (1, 0)]) for part in parts]
-        place = jnp.arange(depth * cores)
-        source = (z - place // cores) % depth + depth * ((place % cores) ^ c)
-    else:
-        parts = [lax.all_gather(jnp.stack(parts), "col", axis=1)]
-        place = jnp.arange(depth * cores)
-        source = (z - place // cores) % depth * cores + place % cores
-    parts = jnp.stack(parts).reshape(depth * cores, *own.shape)
-    return jnp.take(parts, source, axis=0, mode="clip").reshape(-1, own.shape[1])
+    total = None
+    step = max(depth // 2, 1)
+    for first in range(0, depth, step):
+        parts, chunks = [], []
+        if total is not None:
+            rows[first:], total = lax.optimization_barrier((rows[first:], total))
+        for d in range(first, min(first + step, depth)):
+            for e in range(cores):
+                part = rows[d]
+                if e > 0:
+                    part = lax.ppermute(part, "col", [(i, (i + e) % cores) for i in range(cores)])
+                parts.append(part)
+                chunks.append((z - d) % depth * cores + (c - e) % cores)
+        if total is None:
+            total = first_columns(a, parts, chunks)
+        else:
+            total = add_columns(a, parts, chunks, total)
+    return total
 
 
 def columns_t(a, x, depth, cores):
@@ -83,31 +206,25 @@
     which = jnp.stack([lax.axis_index("col"), lax.axis_index("row")]).astype(jnp.int32)
 
     def kernel(which_ref, a_ref, x_ref, out_ref):
-        for e in range(cores):
-            core = lax.rem(which_ref[0] + 1 + e, cores)
-            cols = pl.ds(pl.multiple_of(core * rows, rows), rows)
-            out_ref[e, 0] = matmul_t(a_ref[:, cols], x_ref[...]).astype(BF16)
-
-    return pl.pallas_call(
-        kernel,
-        grid_spec=pltpu.PrefetchScalarGridSpec(
-            num_scalar_prefetch=1,
-            grid=(depth,),
-            in_specs=[
-                pl.BlockSpec(
-                    (k, cores * rows),
-                    lambda d, which_ref: (0, lax.rem(which_ref[1] + d, depth)),
-                ),
-                pl.BlockSpec((k, width), lambda d, which_ref: (0, 0)),
-            ],
-            out_specs=pl.BlockSpec((cores, 1, rows, width), lambda d, which_ref: (0, d, 0, 0)),
-        ),
-        out_shape=jax.ShapeDtypeStruct((cores, depth, rows, width), BF16),
-        compiler_params=pltpu.CompilerParams(vmem_limit_bytes=VMEM),
-        cost_estimate=pl.CostEstimate(
-            flops=2 * k * m * width, bytes_accessed=2 * k * m, transcendentals=0
+        @pl.loop(0, cores * depth)
+        def _(i):
+            core = lax.rem(which_ref[0] + 1 + lax.div(i, depth), cores)
+            z = lax.rem(which_ref[1] + i, depth)
+            cols = pl.ds(pl.multiple_of((z * cores + core) * rows, rows), rows)
+            out_ref[i] = matmul_t(a_ref[:, cols], x_ref[...]).astype(BF16)
+
+    out = pl.pallas_call(
+        kernel,
+        in_specs=[pl.BlockSpec(memory_space=pltpu.SMEM)]
+        + [pl.BlockSpec(memory_space=pltpu.VMEM)] * 2,
+        out_specs=pl.BlockSpec(memory_space=pltpu.VMEM),
+        out_shape=jax.ShapeDtypeStruct((cores * depth, rows, width), BF16),
+        compiler_params=pltpu.CompilerParams(vmem_limit_bytes=RESIDENT),
+        cost_estimate=pl.CostEstimate(
+            flops=2 * k * m * width, bytes_accessed=0, transcendentals=0
         ),
     )(which, a, x)
+    return out.reshape(cores, depth, rows, width)
 
 
 def dot_t(a, x, first, count, tile, dtype):
@@ -146,7 +263,7 @@
     tile = min(m, 1024)
 
     def kernel(a_ref, x_ref, out_ref):
-        out_ref[...] = matmul_t(a_ref[...], x_ref[...])
+        out_ref[...] = matmul_t(a_ref[...], x_ref[...]).astype(BF16)
 
     return pl.pallas_call(
         kernel,
@@ -156,7 +273,7 @@
             pl.BlockSpec((k, width), lambda i: (0, 0)),
         ],
         out_specs=pl.BlockSpec((tile, width), lambda i: (i, 0)),
-        out_shape=jax.ShapeDtypeStruct((m, width), F32),
+        out_shape=jax.ShapeDtypeStruct((m, width), BF16),
         compiler_params=pltpu.CompilerParams(vmem_limit_bytes=VMEM),
         cost_estimate=pl.CostEstimate(
             flops=2 * k * m * width, bytes_accessed=2 * k * m, transcendentals=0
@@ -164,22 +281,18 @@
     )(a, x)
 
 
-def solve_and_swap(a, x):
+def solve_and_scatter(a, x):
+    depth = lax.axis_size("row")
     cores = lax.axis_size("col")
-    parts = columns_t(a, x, lax.axis_size("row"), cores)
-    total = parts[-1]
+    parts = columns_t(a, x, depth, cores)
+    summed = parts[-1]
     for e in range(cores - 1):
-        total = total + lax.ppermute(
+        summed = summed + lax.ppermute(
             parts[e], "col", [(i, (i + 1 + e) % cores) for i in range(cores)]
         )
-    return total
-
-
-def scatter_rows(summed):
-    depth = lax.axis_size("row")
     total = summed[0].astype(F32)
     for d in range(1, depth):
-        moved = lax.ppermute(summed[d], "row", [(i, (i + d) % depth) for i in range(depth)])
+        moved = lax.ppermute(summed[d], "row", [(j, (j + d) % depth) for j in range(depth)])
         total = total + moved.astype(F32)
     return total.astype(BF16)
 
@@ -196,9 +309,10 @@
     middle = [(1, 2), (2, 1)]
 
     def group(first, x):
-        return dot_t(inverse, x, first, GROUP, size, BF16)
+        return dot_t(inverse, x, first, sizes.pop(0), size, BF16)
 
     total = jnp.zeros((width, x.shape[1]), BF16)
+    sizes = list(GROUPS)
     own, outer_got, middle_got = list(group(0, x)), [], []
     for step in range(CHUNKS + 4):
         late = step - 4
@@ -255,8 +369,8 @@
     mine = lax.dynamic_index_in_dim(lists, me, 2, keepdims=False).reshape(-1)
     place = (mine[None, :] == jnp.arange(own, dtype=jnp.int32)[:, None]).astype(BF16)
 
-    forward = sum_cores(matmul(inv_leaf[0], rhs_leaf[0])).astype(BF16)
-    update = matmul(panel[0], forward).astype(BF16).reshape(depth, -1, width)
+    forward = sum_cores(matmul_streamed(inv_leaf[0], rhs_leaf[0], BF16)).astype(BF16)
+    update = matmul_streamed(panel[0], forward, BF16).reshape(depth, -1, width)
     packed = jnp.einsum("bsi,bir->bsr", pick, update, preferred_element_type=F32).astype(BF16)
     packed = packed.reshape(depth, devices, cap, width).transpose(1, 0, 2, 3)
     packed = packed.reshape(devices * per_owner, width)
@@ -266,10 +380,10 @@
     arrived = arrived.reshape(leaves * cores * per_owner, width).astype(BF16)
     reduced = (rhs_parent.astype(F32) - matmul(place, arrived)).astype(BF16)
 
-    whole = gather_block(reduced)
-    halves = swap_leaves(jnp.split(matmul(inv_parent, whole), 2, axis=0), slice(0, None))
+    part = gather_and_solve(inv_parent, reduced)
+    halves = swap_leaves(jnp.split(part, 2, axis=0), slice(0, None))
     fwd_parent = jnp.concatenate(halves, axis=0).astype(BF16)
-    sol_parent = scatter_rows(solve_and_swap(inv_parent, fwd_parent))
+    sol_parent = solve_and_scatter(inv_parent, fwd_parent)
 
     wanted = matmul_t(place, sol_parent).astype(BF16)
     wanted = wanted.reshape(leaves, 1, cores * per_owner, width)

time: 359 us -> 353 us (0.983)
  matrix products: 43.4 us -> 6.24 us
  Pallas kernels: 43 us -> 78.2 us
    dot_general x4 -> x1, matrix products: 37.5 us -> 0.4 us  [matmul(): return jnp.dot(a, x, preferred_element_type=F32)]
    pallas_call x1 -> x5, Pallas kernels: 9.4 us -> 42.7 us  [the longest x2 25.5 us: matmul_streamed(): pl.pallas_call(kernel, in_specs=[pl.BlockSpec(memory_space=pltpu.HBM)] *...]
    unnamed x25 -> x21, local copies, waits for them, and re-layouts: 5.4 us -> 8.06 us
    pallas_call x6 -> x7, Pallas kernels: 24.1 us -> 26 us  [dot_t(): pl.pallas_call(kernel, grid=(count,), in_specs=[pl.BlockSpec((k, tile), l...]
  transfers between devices with their start and end apart: 50 -> 50, of which waited for: 20 -> 22; matrix products, arithmetic and copies ran while one was open for 3% -> 3% of each run, Pallas kernels for 6% -> 8%
where the time goes in v1:
time: 353 us
  waiting for transfers between devices  118 us (33%)
  starting transfers between devices  83.1 us (24%)
  Pallas kernels  78.2 us (22%)
  blocking collectives  41.7 us (12%)
  other arithmetic  12.3 us (3%)
  local copies, waits for them, and re-layouts  11.1 us (3%)
  matrix products  6.24 us (2%)
    ppermute x16, starting transfers between devices, solve_and_sum_rows(): outer_got.append(lax.ppermute(send, 'row', ends))  51 us
    all_to_all x1, blocking collectives, per_device(): lax.all_to_all(wanted.reshape(devices * per_owner, width), ALL, 0, 0, til...  41.7 us
    pallas_call x7, Pallas kernels, dot_t(): pl.pallas_call(kernel, grid=(count,), in_specs=[pl.BlockSpec((k, tile), l...  26 us
    pallas_call x2, Pallas kernels, matmul_streamed(): pl.pallas_call(kernel, in_specs=[pl.BlockSpec(memory_space=pltpu.HBM)] *...  25.5 us
    all_to_all x1, waiting for transfers between devices, per_device(): arrived = lax.all_to_all(packed, ALL, 0, 0, tiled=True)  24.6 us
    ppermute x4, waiting for transfers between devices, swap_leaves(): lax.ppermute(h.astype(BF16), 'leaf', [(i, i ^ order[step]) for i in range...  23.8 us
    ppermute x3, waiting for transfers between devices, solve_and_scatter(): lax.ppermute(summed[d], 'row', [(j, (j + d) % depth) for j in range(depth)])  23.1 us
    ppermute x3, waiting for transfers between devices, gather_and_solve(): lax.ppermute(own, 'row', [(i, (i + d) % depth) for i in range(depth)])  16.4 us
  transfers between devices with their start and end apart: 50, of which 22 were waited for; matrix products, arithmetic and copies ran while one was open for 3% of the time, Pallas kernels for 8%

profile of v1, /device:TPU:0, one launch (start us, length us, event | category | flops | bytes accessed | tf_op | source)
XLA Modules:
  0.0 352.6 jit_solution(8295707471806653595)
XLA Ops:
  0.6 16.3 %shard_map.77 = bf16[3072,256]{1,0:T(8,128)(2,1)S(1)} custom-call(bf16[3072,6144]{1,0:T(8,128)(2,1)} %bitcast.104, bf16[6144,256]{1,0:T(8,128)(2,1)} %bitcast.117), custom_call_target="tpu_custom_call" | custom-call | flops 9663676416 | bytes 37748736 | tf_op jit(solution)/shard_map/pallas_call | solution.py:90
  18.9 2.2 convert_reduce_fusion
  22.7 9.2 %shard_map.78 = bf16[3072,256]{1,0:T(8,128)(2,1)S(1)} custom-call(bf16[3072,3072]{1,0:T(8,128)(2,1)} %bitcast.112, bf16[3072,256]{1,0:T(8,128)(2,1)} %add_convert_fusion.x_ref), custom_call_target="tpu_custom_call" | custom-call | flops 4831838208 | bytes 18874368 | tf_op jit(solution)/shard_map/pallas_call | solution.py:90
  31.9 3.4 fusion.4
  36.7 7.0 %all-to-all-start = ((bf16[32,96,256]{2,1,0:T(8,128)(2,1)}), bf16[32,96,256]{2,1,0:T(8,128)(2,1)S(1)}, u32[]{:S(2)}, u32[]{:S(2)}) async-start(bf16[32,96,256]{2,1,0:T(8,128)(2,1)} %bitcast.19), calls=%async_computation | async-start | bytes 3145728 | tf_op jit(solution)/shard_map/all_to_all | solution.py:378
  43.6 1.7 select_reduce_fusion
  45.6 2.7 collective-permute-start.3
  49.3 6.6 %collective-permute-done.3 = s32[32,96]{1,0:T(8,128)S(1)} collective-permute-done((s32[32,96]{1,0:T(8,128)S(1)}, s32[32,96]{1,0:T(8,128)S(1)}, u32[]{:S(2)}, u32[]{:S(2)}) %collective-permute-start.3) | collective-permute-done | bytes 12320 | tf_op jit(solution)/shard_map/ppermute | solution.py:48
  57.9 24.6 %all-to-all-done = bf16[32,96,256]{2,1,0:T(8,128)(2,1)S(1)} async-done(((bf16[32,96,256]{2,1,0:T(8,128)(2,1)}), bf16[32,96,256]{2,1,0:T(8,128)(2,1)S(1)}, u32[]{:S(2)}, u32[]{:S(2)}) %all-to-all-start) | async-done | bytes 1572896 | tf_op jit(solution)/shard_map/all_to_all | solution.py:378
  83.5 9.6 %collective-permute-done.8.refs_2_ = bf16[512,256]{1,0:T(8,128)(2,1)S(1)} collective-permute-done((bf16[512,256]{1,0:T(8,128)(2,1)S(1)}, bf16[512,256]{1,0:T(8,128)(2,1)S(1)}, u32[]{:S(2)}, u32[]{:S(2)}) %collective-permute-start.8) | collective-permute-done | bytes 262176 | tf_op jit(solution)/shard_map/ppermute | solution.py:179
  94.6 6.1 %shard_map.79.refs_4_ = f32[2048,256]{1,0:T(8,128)S(1)} custom-call(s32[4]{0:T(128)S(1)} %pad_add_fusion.3.chunks_ref, bf16[2048,4096]{1,0:T(8,128)(2,1)} %a_ref.5, bf16[512,256]{1,0:T(8,128)(2,1)S(1)} %fusion.10.refs_0_, bf16[512,256]{1,0:T(8,128)(2,1)S(1)} %collective-permute-done.7.refs_1_, bf16[512,256]{1,0:T(8,128)(2,1)S(1)} %collective-permute-done.8.refs_2_, ...), custom_call_target="tpu_custom_call" | custom-call | flops 2147483648 | bytes 16777216 | tf_op jit(solution)/shard_map/pallas_call | solution.py:154
  100.7 5.6 %collective-permute-done.5.refs_0_ = bf16[512,256]{1,0:T(8,128)(2,1)S(1)} collective-permute-done((bf16[512,256]{1,0:T(8,128)(2,1)S(1)}, bf16[512,256]{1,0:T(8,128)(2,1)S(1)}, u32[]{:S(2)}, u32[]{:S(2)}) %collective-permute-start.5) | collective-permute-done | bytes 262176 | tf_op jit(solution)/shard_map/ppermute | solution.py:179
  109.6 5.8 %copy-done = bf16[2048,4096]{1,0:T(8,128)(2,1)S(1)} copy-done((bf16[2048,4096]{1,0:T(8,128)(2,1)S(1)}, bf16[2048,4096]{1,0:T(8,128)(2,1)}, u32[]{:S(2)}) %copy-start) | copy-done | bytes 16777240
  115.4 4.0 %shard_map.80 = f32[2048,256]{1,0:T(8,128)S(1)} custom-call(s32[4]{0:T(128)S(1)} %pad_add_fusion.2.chunks_ref, bf16[2048,4096]{1,0:T(8,128)(2,1)S(1)} %copy-done, bf16[512,256]{1,0:T(8,128)(2,1)S(1)} %collective-permute-done.5.refs_0_, bf16[512,256]{1,0:T(8,128)(2,1)S(1)} %collective-permute-done.10.refs_1_, ...), custom_call_target="tpu_custom_call" | custom-call | flops 2147483648 | tf_op jit(solution)/shard_map/pallas_call | solution.py:127
  121.3 12.3 %collective-permute-done.12 = bf16[1024,256]{1,0:T(8,128)(2,1)S(1)} collective-permute-done((bf16[1024,256]{1,0:T(8,128)(2,1)S(1)}, bf16[1024,256]{1,0:T(8,128)(2,1)S(1)}, u32[]{:S(2)}, u32[]{:S(2)}) %collective-permute-start.12) | collective-permute-done | bytes 524320 | tf_op jit(solution)/shard_map/ppermute | solution.py:38
  137.0 10.3 %collective-permute-done.13 = bf16[1024,256]{1,0:T(8,128)(2,1)S(1)} collective-permute-done((bf16[1024,256]{1,0:T(8,128)(2,1)S(1)}, bf16[1024,256]{1,0:T(8,128)(2,1)S(1)}, u32[]{:S(2)}, u32[]{:S(2)}) %collective-permute-start.13) | collective-permute-done | bytes 524320 | tf_op jit(solution)/shard_map/ppermute | solution.py:38
  148.6 7.2 %shard_map.81 = bf16[8,512,256]{2,1,0:T(8,128)(2,1)S(1)} custom-call(s32[2]{0:T(128)S(1)} %pad_add_fusion.1.which_ref, bf16[2048,4096]{1,0:T(8,128)(2,1)S(1)} %bitcast.101, bf16[2048,256]{1,0:T(8,128)(2,1)S(1)} %pad_maximum_fusion.x_ref), custom_call_target="tpu_custom_call" | custom-call | flops 4294967296 | tf_op jit(solution)/shard_map/pallas_call | solution.py:216
  155.9 2.6 collective-permute-done.16
  158.8 6.0 %collective-permute-start.19 = (bf16[512,256]{1,0:T(8,128)(2,1)S(1)}, bf16[512,256]{1,0:T(8,128)(2,1)S(1)}, u32[]{:S(2)}, u32[]{:S(2)}) collective-permute-start(bf16[512,256]{1,0:T(8,128)(2,1)S(1)} %get-tuple-element.131), channel_id=1, source_target_pairs={{0,6},{2,0},{4,2},{6,4},{1,7},{3,1},{5,3},{7,5},{8,14},{10,8},{12,... | collective-permute-start | bytes 786440 | tf_op jit(solution)/shard_map/ppermute | solution.py:295
  165.4 6.1 %collective-permute-done.19 = bf16[512,256]{1,0:T(8,128)(2,1)S(1)} collective-permute-done((bf16[512,256]{1,0:T(8,128)(2,1)S(1)}, bf16[512,256]{1,0:T(8,128)(2,1)S(1)}, u32[]{:S(2)}, u32[]{:S(2)}) %collective-permute-start.19) | collective-permute-done | bytes 262176 | tf_op jit(solution)/shard_map/ppermute | solution.py:295
  171.5 17.0 %collective-permute-done.18 = bf16[512,256]{1,0:T(8,128)(2,1)S(1)} collective-permute-done((bf16[512,256]{1,0:T(8,128)(2,1)S(1)}, bf16[512,256]{1,0:T(8,128)(2,1)S(1)}, u32[]{:S(2)}, u32[]{:S(2)}) %collective-permute-start.18) | collective-permute-done | bytes 262176 | tf_op jit(solution)/shard_map/ppermute | solution.py:295
  189.5 41.7 %all_to_all.18 = bf16[32,96,256]{2,1,0:T(8,128)(2,1)S(1)} all-to-all(bf16[32,96,256]{2,1,0:T(8,128)(2,1)S(1)} %bitcast.116), channel_id=1, replica_groups=mesh['leaf'=4,'row'=4,'col'=2] {'leaf','row','col'}, dimensions={0} | all-to-all | bytes 3145728 | tf_op jit(solution)/shard_map/all_to_all | solution.py:391
  231.3 1.9 fusion.5
  233.3 9.5 %shard_map.82 = bf16[3072,256]{1,0:T(8,128)(2,1)S(1)} custom-call(bf16[3072,3072]{1,0:T(8,128)(2,1)} %bitcast.113, bf16[3072,256]{1,0:T(8,128)(2,1)S(1)} %bitcast.102), custom_call_target="tpu_custom_call" | custom-call | flops 4831838208 | bytes 18874368 | tf_op jit(solution)/shard_map/pallas_call | solution.py:268
  242.9 3.4 collective-permute-done.20
  246.8 2.9 shard_map.83
  249.8 2.9 shard_map.84
  252.8 2.1 collective-permute-start.23
  254.8 4.0 %shard_map.85 = (bf16[512,256]{1,0:T(8,128)(2,1)S(1)}, bf16[512,256]{1,0:T(8,128)(2,1)S(1)}) custom-call(bf16[3072,6144]{1,0:T(8,128)(2,1)} %bitcast.107, bf16[3072,256]{1,0:T(8,128)(2,1)S(1)} %subtract_convert_fusion.x_ref), custom_call_target="tpu_custom_call" | custom-call | flops 1610612736 | bytes 6291456 | tf_op jit(solution)/shard_map/pallas_call | solution.py:242
  260.4 3.4 collective-permute-done.23
  264.9 4.0 %shard_map.86 = (bf16[512,256]{1,0:T(8,128)(2,1)S(1)}, bf16[512,256]{1,0:T(8,128)(2,1)S(1)}) custom-call(bf16[3072,6144]{1,0:T(8,128)(2,1)} %bitcast.108, bf16[3072,256]{1,0:T(8,128)(2,1)S(1)} %subtract_convert_fusion.x_ref), custom_call_target="tpu_custom_call" | custom-call | flops 1610612736 | bytes 6291456 | tf_op jit(solution)/shard_map/pallas_call | solution.py:242
  268.9 3.0 collective-permute-start.27
  272.2 7.0 %collective-permute-done.27 = bf16[512,256]{1,0:T(8,128)(2,1)S(1)} collective-permute-done((bf16[512,256]{1,0:T(8,128)(2,1)S(1)}, bf16[512,256]{1,0:T(8,128)(2,1)S(1)}, u32[]{:S(2)}, u32[]{:S(2)}) %collective-permute-start.27) | collective-permute-done | bytes 262176 | tf_op jit(solution)/shard_map/ppermute | solution.py:333
  279.2 2.1 collective-permute-start.28
  282.7 4.0 %shard_map.87 = (bf16[512,256]{1,0:T(8,128)(2,1)S(1)}, bf16[512,256]{1,0:T(8,128)(2,1)S(1)}) custom-call(bf16[3072,6144]{1,0:T(8,128)(2,1)} %bitcast.109, bf16[3072,256]{1,0:T(8,128)(2,1)S(1)} %subtract_convert_fusion.x_ref), custom_call_target="tpu_custom_call" | custom-call | flops 1610612736 | bytes 6291456 | tf_op jit(solution)/shard_map/pallas_call | solution.py:242
  287.2 4.6 %collective-permute-start.30 = (bf16[512,256]{1,0:T(8,128)(2,1)S(1)}, bf16[512,256]{1,0:T(8,128)(2,1)S(1)}, u32[]{:S(2)}, u32[]{:S(2)}) collective-permute-start(bf16[512,256]{1,0:T(8,128)(2,1)S(1)} %add_select_fusion.5), channel_id=1, source_target_pairs={{0,2},{2,0},{4,6},{6,4},{1,3},{3,1},{5,7},{7,5},{8,10},{10,8},{12,... | collective-permute-start | bytes 786440 | tf_op jit(solution)/shard_map/ppermute | solution.py:333
  291.9 1.9 collective-permute-start.32
  295.6 4.0 %shard_map.88 = (bf16[512,256]{1,0:T(8,128)(2,1)S(1)}, bf16[512,256]{1,0:T(8,128)(2,1)S(1)}) custom-call(bf16[3072,6144]{1,0:T(8,128)(2,1)} %bitcast.110, bf16[3072,256]{1,0:T(8,128)(2,1)S(1)} %subtract_convert_fusion.x_ref), custom_call_target="tpu_custom_call" | custom-call | flops 1610612736 | bytes 6291456 | tf_op jit(solution)/shard_map/pallas_call | solution.py:242
  299.8 4.8 %collective-permute-start.34 = (bf16[512,256]{1,0:T(8,128)(2,1)S(1)}, bf16[512,256]{1,0:T(8,128)(2,1)S(1)}, u32[]{:S(2)}, u32[]{:S(2)}) collective-permute-start(bf16[512,256]{1,0:T(8,128)(2,1)S(1)} %add_select_fusion.3), channel_id=1, source_target_pairs={{0,2},{2,0},{4,6},{6,4},{1,3},{3,1},{5,7},{7,5},{8,10},{10,8},{12,... | collective-permute-start | bytes 786440 | tf_op jit(solution)/shard_map/ppermute | solution.py:333
  304.7 2.2 collective-permute-start.36
  308.5 4.0 %shard_map.89 = (bf16[512,256]{1,0:T(8,128)(2,1)S(1)}, bf16[512,256]{1,0:T(8,128)(2,1)S(1)}) custom-call(bf16[3072,6144]{1,0:T(8,128)(2,1)} %bitcast.111, bf16[3072,256]{1,0:T(8,128)(2,1)S(1)} %subtract_convert_fusion.x_ref), custom_call_target="tpu_custom_call" | custom-call | flops 1610612736 | bytes 6291456 | tf_op jit(solution)/shard_map/pallas_call | solution.py:242
  312.6 4.6 %collective-permute-start.38 = (bf16[512,256]{1,0:T(8,128)(2,1)S(1)}, bf16[512,256]{1,0:T(8,128)(2,1)S(1)}, u32[]{:S(2)}, u32[]{:S(2)}) collective-permute-start(bf16[512,256]{1,0:T(8,128)(2,1)S(1)} %add_select_fusion.1), channel_id=1, source_target_pairs={{0,2},{2,0},{4,6},{6,4},{1,3},{3,1},{5,7},{7,5},{8,10},{10,8},{12,... | collective-permute-start | bytes 786440 | tf_op jit(solution)/shard_map/ppermute | solution.py:333
  317.4 3.5 collective-permute-start.40
  322.7 6.7 %collective-permute-start.42 = (bf16[512,256]{1,0:T(8,128)(2,1)S(1)}, bf16[512,256]{1,0:T(8,128)(2,1)S(1)}, u32[]{:S(2)}, u32[]{:S(2)}) collective-permute-start(bf16[512,256]{1,0:T(8,128)(2,1)S(1)} %add.336), channel_id=1, source_target_pairs={{0,2},{2,0},{4,6},{6,4},{1,3},{3,1},{5,7},{7,5},{8,10},{10,8},{12,... | collective-permute-start | bytes 786440 | tf_op jit(solution)/shard_map/ppermute | solution.py:333
  329.5 5.2 %collective-permute-start.44 = (bf16[512,256]{1,0:T(8,128)(2,1)S(1)}, bf16[512,256]{1,0:T(8,128)(2,1)S(1)}, u32[]{:S(2)}, u32[]{:S(2)}) collective-permute-start(bf16[512,256]{1,0:T(8,128)(2,1)S(1)} %add.340), channel_id=1, source_target_pairs={{0,2},{2,0},{4,6},{6,4},{1,3},{3,1},{5,7},{7,5},{8,10},{10,8},{12,... | collective-permute-start | bytes 786440 | tf_op jit(solution)/shard_map/ppermute | solution.py:333
  336.4 6.7 %collective-permute-start.46 = (bf16[512,256]{1,0:T(8,128)(2,1)S(1)}, bf16[512,256]{1,0:T(8,128)(2,1)S(1)}, u32[]{:S(2)}, u32[]{:S(2)}) collective-permute-start(bf16[512,256]{1,0:T(8,128)(2,1)S(1)} %add.344), channel_id=1, source_target_pairs={{0,2},{2,0},{4,6},{6,4},{1,3},{3,1},{5,7},{7,5},{8,10},{10,8},{12,... | collective-permute-start | bytes 786440 | tf_op jit(solution)/shard_map/ppermute | solution.py:333
  343.2 3.3 collective-permute-start.48
  347.6 3.2 collective-permute-done.48
  (165 shorter events, 38.3 us)
Async XLA Ops:
  17.0 4.2 %collective-permute-start = (bf16[3072,256]{1,0:T(8,128)(2,1)S(1)}, bf16[3072,256]{1,0:T(8,128)(2,1)S(1)}, u32[]{:S(2)}, u32[]{:S(2)}) collective-permute-start(bf16[3072,256]{1,0:T(8,128)(2,1)S(1)} %shard_map.77), channel_id=1, source_target_pairs={{0,1},{1,0},{2,3},{3,2},{4,5},{5,4},{6,7},{7,6},{8,9},{9,8},{10,11... | collective-permute-start | bytes 4718600 | tf_op jit(solution)/shard_map/ppermute | solution.py:27
  36.7 45.8 %all-to-all-start = ((bf16[32,96,256]{2,1,0:T(8,128)(2,1)}), bf16[32,96,256]{2,1,0:T(8,128)(2,1)S(1)}, u32[]{:S(2)}, u32[]{:S(2)}) async-start(bf16[32,96,256]{2,1,0:T(8,128)(2,1)} %bitcast.19), calls=%async_computation | async-start | bytes 3145728 | tf_op jit(solution)/shard_map/all_to_all | solution.py:378
  45.6 10.3 %collective-permute-start.3 = (s32[32,96]{1,0:T(8,128)S(1)}, s32[32,96]{1,0:T(8,128)S(1)}, u32[]{:S(2)}, u32[]{:S(2)}) collective-permute-start(s32[32,96]{1,0:T(8,128)S(1)} %reshape.183), channel_id=1, source_target_pairs={{0,24},{8,16},{16,8},{24,0},{1,25},{9,17},{17,9},{25,1},{2,26},{10... | collective-permute-start | bytes 36872 | tf_op jit(solution)/shard_map/ppermute | solution.py:48
  48.3 7.6 %collective-permute-start.2 = (s32[32,96]{1,0:T(8,128)S(1)}, s32[32,96]{1,0:T(8,128)S(1)}, u32[]{:S(2)}, u32[]{:S(2)}) collective-permute-start(s32[32,96]{1,0:T(8,128)S(1)} %reshape.183), channel_id=1, source_target_pairs={{0,16},{8,24},{16,0},{24,8},{1,17},{9,25},{17,1},{25,9},{2,18},{10... | collective-permute-start | bytes 36872 | tf_op jit(solution)/shard_map/ppermute | solution.py:48
  48.9 7.0 %collective-permute-start.1 = (s32[32,96]{1,0:T(8,128)S(1)}, s32[32,96]{1,0:T(8,128)S(1)}, u32[]{:S(2)}, u32[]{:S(2)}) collective-permute-start(s32[32,96]{1,0:T(8,128)S(1)} %reshape.183), channel_id=1, source_target_pairs={{0,8},{8,0},{16,24},{24,16},{1,9},{9,1},{17,25},{25,17},{2,10},{10... | collective-permute-start | bytes 36872 | tf_op jit(solution)/shard_map/ppermute | solution.py:48
  83.3 9.7 %collective-permute-start.8 = (bf16[512,256]{1,0:T(8,128)(2,1)S(1)}, bf16[512,256]{1,0:T(8,128)(2,1)S(1)}, u32[]{:S(2)}, u32[]{:S(2)}) collective-permute-start(bf16[512,256]{1,0:T(8,128)(2,1)S(1)} %fusion.10.refs_0_), channel_id=1, source_target_pairs={{0,2},{2,4},{4,6},{6,0},{1,3},{3,5},{5,7},{7,1},{8,10},{10,12},{12... | collective-permute-start | bytes 786440 | tf_op jit(solution)/shard_map/ppermute | solution.py:179
  83.4 10.6 %collective-permute-start.7 = (bf16[512,256]{1,0:T(8,128)(2,1)S(1)}, bf16[512,256]{1,0:T(8,128)(2,1)S(1)}, u32[]{:S(2)}, u32[]{:S(2)}) collective-permute-start(bf16[512,256]{1,0:T(8,128)(2,1)S(1)} %fusion.10.refs_0_), channel_id=1, source_target_pairs={{0,1},{1,0},{2,3},{3,2},{4,5},{5,4},{6,7},{7,6},{8,9},{9,8},{10,11... | collective-permute-start | bytes 786440 | tf_op jit(solution)/shard_map/ppermute | solution.py:192
  93.1 13.3 %collective-permute-start.5 = (bf16[512,256]{1,0:T(8,128)(2,1)S(1)}, bf16[512,256]{1,0:T(8,128)(2,1)S(1)}, u32[]{:S(2)}, u32[]{:S(2)}) collective-permute-start(bf16[512,256]{1,0:T(8,128)(2,1)S(1)} %fusion.10.refs_0_), channel_id=1, source_target_pairs={{0,4},{2,6},{4,0},{6,2},{1,5},{3,7},{5,1},{7,3},{8,12},{10,14},{12... | collective-permute-start | bytes 786440 | tf_op jit(solution)/shard_map/ppermute | solution.py:179
  93.1 14.4 %collective-permute-start.6 = (bf16[512,256]{1,0:T(8,128)(2,1)S(1)}, bf16[512,256]{1,0:T(8,128)(2,1)}, u32[]{:S(2)}, u32[]{:S(2)}) collective-permute-start(bf16[512,256]{1,0:T(8,128)(2,1)S(1)} %fusion.10.refs_0_), channel_id=1, source_target_pairs={{0,6},{2,0},{4,2},{6,4},{1,7},{3,1},{5,3},{7,5},{8,14},{10,8},{12,... | collective-permute-start | bytes 786440 | tf_op jit(solution)/shard_map/ppermute | solution.py:179
  107.5 1.9 collective-permute-start.10
  107.5 2.1 collective-permute-start.11
  119.5 14.1 %collective-permute-start.12 = (bf16[1024,256]{1,0:T(8,128)(2,1)S(1)}, bf16[1024,256]{1,0:T(8,128)(2,1)S(1)}, u32[]{:S(2)}, u32[]{:S(2)}) collective-permute-start(bf16[1024,256]{1,0:T(8,128)(2,1)S(1)} %get-tuple-element.128), channel_id=1, source_target_pairs={{0,8},{8,0},{16,24},{24,16},{1,9},{9,1},{17,25},{25,17},{2,10},{10... | collective-permute-start | bytes 1572872 | tf_op jit(solution)/shard_map/ppermute | solution.py:38
  120.3 13.7 %collective-permute-start.14 = (bf16[1024,256]{1,0:T(8,128)(2,1)S(1)}, bf16[1024,256]{1,0:T(8,128)(2,1)S(1)}, u32[]{:S(2)}, u32[]{:S(2)}) collective-permute-start(bf16[1024,256]{1,0:T(8,128)(2,1)S(1)} %get-tuple-element.129), channel_id=1, source_target_pairs={{0,16},{8,24},{16,0},{24,8},{1,17},{9,25},{17,1},{25,9},{2,18},{10... | collective-permute-start | bytes 1572872 | tf_op jit(solution)/shard_map/ppermute | solution.py:38
  134.3 12.9 %collective-permute-start.13 = (bf16[1024,256]{1,0:T(8,128)(2,1)S(1)}, bf16[1024,256]{1,0:T(8,128)(2,1)S(1)}, u32[]{:S(2)}, u32[]{:S(2)}) collective-permute-start(bf16[1024,256]{1,0:T(8,128)(2,1)S(1)} %get-tuple-element.126), channel_id=1, source_target_pairs={{0,16},{8,24},{16,0},{24,8},{1,17},{9,25},{17,1},{25,9},{2,18},{10... | collective-permute-start | bytes 1572872 | tf_op jit(solution)/shard_map/ppermute | solution.py:38
  135.4 12.7 %collective-permute-start.15 = (bf16[1024,256]{1,0:T(8,128)(2,1)S(1)}, bf16[1024,256]{1,0:T(8,128)(2,1)S(1)}, u32[]{:S(2)}, u32[]{:S(2)}) collective-permute-start(bf16[1024,256]{1,0:T(8,128)(2,1)S(1)} %get-tuple-element.127), channel_id=1, source_target_pairs={{0,8},{8,0},{16,24},{24,16},{1,9},{9,1},{17,25},{25,17},{2,10},{10... | collective-permute-start | bytes 1572872 | tf_op jit(solution)/shard_map/ppermute | solution.py:38
  155.8 2.7 collective-permute-start.16
  158.8 12.8 %collective-permute-start.19 = (bf16[512,256]{1,0:T(8,128)(2,1)S(1)}, bf16[512,256]{1,0:T(8,128)(2,1)S(1)}, u32[]{:S(2)}, u32[]{:S(2)}) collective-permute-start(bf16[512,256]{1,0:T(8,128)(2,1)S(1)} %get-tuple-element.131), channel_id=1, source_target_pairs={{0,6},{2,0},{4,2},{6,4},{1,7},{3,1},{5,3},{7,5},{8,14},{10,8},{12,... | collective-permute-start | bytes 786440 | tf_op jit(solution)/shard_map/ppermute | solution.py:295
  164.8 23.7 %collective-permute-start.18 = (bf16[512,256]{1,0:T(8,128)(2,1)S(1)}, bf16[512,256]{1,0:T(8,128)(2,1)S(1)}, u32[]{:S(2)}, u32[]{:S(2)}) collective-permute-start(bf16[512,256]{1,0:T(8,128)(2,1)S(1)} %get-tuple-element.132), channel_id=1, source_target_pairs={{0,4},{2,6},{4,0},{6,2},{1,5},{3,7},{5,1},{7,3},{8,12},{10,14},{12... | collective-permute-start | bytes 786440 | tf_op jit(solution)/shard_map/ppermute | solution.py:295
  165.3 23.2 %collective-permute-start.17 = (bf16[512,256]{1,0:T(8,128)(2,1)S(1)}, bf16[512,256]{1,0:T(8,128)(2,1)S(1)}, u32[]{:S(2)}, u32[]{:S(2)}) collective-permute-start(bf16[512,256]{1,0:T(8,128)(2,1)S(1)} %get-tuple-element.130), channel_id=1, source_target_pairs={{0,2},{2,4},{4,6},{6,0},{1,3},{3,5},{5,7},{7,1},{8,10},{10,12},{12... | collective-permute-start | bytes 786440 | tf_op jit(solution)/shard_map/ppermute | solution.py:295
  242.8 3.5 collective-permute-start.20
  249.8 9.2 %collective-permute-start.21 = (bf16[512,256]{1,0:T(8,128)(2,1)S(1)}, bf16[512,256]{1,0:T(8,128)(2,1)S(1)}, u32[]{:S(2)}, u32[]{:S(2)}) collective-permute-start(bf16[512,256]{1,0:T(8,128)(2,1)S(1)} %shard_map.83), channel_id=1, source_target_pairs={{0,2},{2,0},{4,6},{6,4},{1,3},{3,1},{5,7},{7,5},{8,10},{10,8},{12,... | collective-permute-start | bytes 786440 | tf_op jit(solution)/shard_map/ppermute | solution.py:333
  252.8 11.0 %collective-permute-start.23 = (bf16[512,256]{1,0:T(8,128)(2,1)S(1)}, bf16[512,256]{1,0:T(8,128)(2,1)S(1)}, u32[]{:S(2)}, u32[]{:S(2)}) collective-permute-start(bf16[512,256]{1,0:T(8,128)(2,1)S(1)} %shard_map.84), channel_id=1, source_target_pairs={{0,2},{2,0},{4,6},{6,4},{1,3},{3,1},{5,7},{7,5},{8,10},{10,8},{12,... | collective-permute-start | bytes 786440 | tf_op jit(solution)/shard_map/ppermute | solution.py:333
  259.7 12.2 %collective-permute-start.22 = (bf16[512,256]{1,0:T(8,128)(2,1)}, bf16[512,256]{1,0:T(8,128)(2,1)S(1)}, u32[]{:S(2)}, u32[]{:S(2)}) collective-permute-start(bf16[512,256]{1,0:T(8,128)(2,1)} %add.301), channel_id=1, source_target_pairs={{2,4},{4,2},{3,5},{5,3},{10,12},{12,10},{11,13},{13,11},{18,20},{2... | collective-permute-start | bytes 786440 | tf_op jit(solution)/shard_map/ppermute | solution.py:329
  263.9 8.2 %collective-permute-start.24 = (bf16[512,256]{1,0:T(8,128)(2,1)S(1)}, bf16[512,256]{1,0:T(8,128)(2,1)S(1)}, u32[]{:S(2)}, u32[]{:S(2)}) collective-permute-start(bf16[512,256]{1,0:T(8,128)(2,1)S(1)} %get-tuple-element.77), channel_id=1, source_target_pairs={{0,2},{2,0},{4,6},{6,4},{1,3},{3,1},{5,7},{7,5},{8,10},{10,8},{12,... | collective-permute-start | bytes 786440 | tf_op jit(solution)/shard_map/ppermute | solution.py:333
  264.2 8.0 %collective-permute-start.26 = (bf16[512,256]{1,0:T(8,128)(2,1)S(1)}, bf16[512,256]{1,0:T(8,128)(2,1)S(1)}, u32[]{:S(2)}, u32[]{:S(2)}) collective-permute-start(bf16[512,256]{1,0:T(8,128)(2,1)S(1)} %add.304), channel_id=1, source_target_pairs={{2,4},{4,2},{3,5},{5,3},{10,12},{12,10},{11,13},{13,11},{18,20},{2... | collective-permute-start | bytes 786440 | tf_op jit(solution)/shard_map/ppermute | solution.py:329
  268.9 10.3 %collective-permute-start.27 = (bf16[512,256]{1,0:T(8,128)(2,1)S(1)}, bf16[512,256]{1,0:T(8,128)(2,1)S(1)}, u32[]{:S(2)}, u32[]{:S(2)}) collective-permute-start(bf16[512,256]{1,0:T(8,128)(2,1)S(1)} %get-tuple-element.82), channel_id=1, source_target_pairs={{0,2},{2,0},{4,6},{6,4},{1,3},{3,1},{5,7},{7,5},{8,10},{10,8},{12,... | collective-permute-start | bytes 786440 | tf_op jit(solution)/shard_map/ppermute | solution.py:333
  272.1 14.6 %collective-permute-start.25 = (bf16[512,256]{1,0:T(8,128)(2,1)S(1)}, bf16[512,256]{1,0:T(8,128)(2,1)S(1)}, u32[]{:S(2)}, u32[]{:S(2)}) collective-permute-start(bf16[512,256]{1,0:T(8,128)(2,1)S(1)} %add_select_fusion.7), channel_id=1, source_target_pairs={{0,2},{2,0},{4,6},{6,4},{1,3},{3,1},{5,7},{7,5},{8,10},{10,8},{12,... | collective-permute-start | bytes 786440 | tf_op jit(solution)/shard_map/ppermute | solution.py:333
  279.2 12.6 %collective-permute-start.28 = (bf16[512,256]{1,0:T(8,128)(2,1)S(1)}, bf16[512,256]{1,0:T(8,128)(2,1)S(1)}, u32[]{:S(2)}, u32[]{:S(2)}) collective-permute-start(bf16[512,256]{1,0:T(8,128)(2,1)S(1)} %add_select_fusion.6), channel_id=1, source_target_pairs={{0,2},{2,0},{4,6},{6,4},{1,3},{3,1},{5,7},{7,5},{8,10},{10,8},{12,... | collective-permute-start | bytes 786440 | tf_op jit(solution)/shard_map/ppermute | solution.py:333
  281.3 5.8 %collective-permute-start.29 = (bf16[512,256]{1,0:T(8,128)(2,1)S(1)}, bf16[512,256]{1,0:T(8,128)(2,1)S(1)}, u32[]{:S(2)}, u32[]{:S(2)}) collective-permute-start(bf16[512,256]{1,0:T(8,128)(2,1)S(1)} %add.305), channel_id=1, source_target_pairs={{2,4},{4,2},{3,5},{5,3},{10,12},{12,10},{11,13},{13,11},{18,20},{2... | collective-permute-start | bytes 786440 | tf_op jit(solution)/shard_map/ppermute | solution.py:329
  282.0 9.9 %collective-permute-start.31 = (bf16[512,256]{1,0:T(8,128)(2,1)S(1)}, bf16[512,256]{1,0:T(8,128)(2,1)S(1)}, u32[]{:S(2)}, u32[]{:S(2)}) collective-permute-start(bf16[512,256]{1,0:T(8,128)(2,1)S(1)} %add.309), channel_id=1, source_target_pairs={{2,4},{4,2},{3,5},{5,3},{10,12},{12,10},{11,13},{13,11},{18,20},{2... | collective-permute-start | bytes 786440 | tf_op jit(solution)/shard_map/ppermute | solution.py:329
  287.2 12.4 %collective-permute-start.30 = (bf16[512,256]{1,0:T(8,128)(2,1)S(1)}, bf16[512,256]{1,0:T(8,128)(2,1)S(1)}, u32[]{:S(2)}, u32[]{:S(2)}) collective-permute-start(bf16[512,256]{1,0:T(8,128)(2,1)S(1)} %add_select_fusion.5), channel_id=1, source_target_pairs={{0,2},{2,0},{4,6},{6,4},{1,3},{3,1},{5,7},{7,5},{8,10},{10,8},{12,... | collective-permute-start | bytes 786440 | tf_op jit(solution)/shard_map/ppermute | solution.py:333
  291.9 12.6 %collective-permute-start.32 = (bf16[512,256]{1,0:T(8,128)(2,1)S(1)}, bf16[512,256]{1,0:T(8,128)(2,1)S(1)}, u32[]{:S(2)}, u32[]{:S(2)}) collective-permute-start(bf16[512,256]{1,0:T(8,128)(2,1)S(1)} %add_select_fusion.4), channel_id=1, source_target_pairs={{0,2},{2,0},{4,6},{6,4},{1,3},{3,1},{5,7},{7,5},{8,10},{10,8},{12,... | collective-permute-start | bytes 786440 | tf_op jit(solution)/shard_map/ppermute | solution.py:333
  293.8 5.9 %collective-permute-start.33 = (bf16[512,256]{1,0:T(8,128)(2,1)S(1)}, bf16[512,256]{1,0:T(8,128)(2,1)S(1)}, u32[]{:S(2)}, u32[]{:S(2)}) collective-permute-start(bf16[512,256]{1,0:T(8,128)(2,1)S(1)} %add.313), channel_id=1, source_target_pairs={{2,4},{4,2},{3,5},{5,3},{10,12},{12,10},{11,13},{13,11},{18,20},{2... | collective-permute-start | bytes 786440 | tf_op jit(solution)/shard_map/ppermute | solution.py:329
  294.5 10.1 %collective-permute-start.35 = (bf16[512,256]{1,0:T(8,128)(2,1)S(1)}, bf16[512,256]{1,0:T(8,128)(2,1)S(1)}, u32[]{:S(2)}, u32[]{:S(2)}) collective-permute-start(bf16[512,256]{1,0:T(8,128)(2,1)S(1)} %add.317), channel_id=1, source_target_pairs={{2,4},{4,2},{3,5},{5,3},{10,12},{12,10},{11,13},{13,11},{18,20},{2... | collective-permute-start | bytes 786440 | tf_op jit(solution)/shard_map/ppermute | solution.py:329
  299.8 12.8 %collective-permute-start.34 = (bf16[512,256]{1,0:T(8,128)(2,1)S(1)}, bf16[512,256]{1,0:T(8,128)(2,1)S(1)}, u32[]{:S(2)}, u32[]{:S(2)}) collective-permute-start(bf16[512,256]{1,0:T(8,128)(2,1)S(1)} %add_select_fusion.3), channel_id=1, source_target_pairs={{0,2},{2,0},{4,6},{6,4},{1,3},{3,1},{5,7},{7,5},{8,10},{10,8},{12,... | collective-permute-start | bytes 786440 | tf_op jit(solution)/shard_map/ppermute | solution.py:333
  304.7 12.6 %collective-permute-start.36 = (bf16[512,256]{1,0:T(8,128)(2,1)S(1)}, bf16[512,256]{1,0:T(8,128)(2,1)S(1)}, u32[]{:S(2)}, u32[]{:S(2)}) collective-permute-start(bf16[512,256]{1,0:T(8,128)(2,1)S(1)} %add_select_fusion.2), channel_id=1, source_target_pairs={{0,2},{2,0},{4,6},{6,4},{1,3},{3,1},{5,7},{7,5},{8,10},{10,8},{12,... | collective-permute-start | bytes 786440 | tf_op jit(solution)/shard_map/ppermute | solution.py:333
  306.8 5.8 %collective-permute-start.37 = (bf16[512,256]{1,0:T(8,128)(2,1)S(1)}, bf16[512,256]{1,0:T(8,128)(2,1)S(1)}, u32[]{:S(2)}, u32[]{:S(2)}) collective-permute-start(bf16[512,256]{1,0:T(8,128)(2,1)S(1)} %add.321), channel_id=1, source_target_pairs={{2,4},{4,2},{3,5},{5,3},{10,12},{12,10},{11,13},{13,11},{18,20},{2... | collective-permute-start | bytes 786440 | tf_op jit(solution)/shard_map/ppermute | solution.py:329
  307.5 9.8 %collective-permute-start.39 = (bf16[512,256]{1,0:T(8,128)(2,1)S(1)}, bf16[512,256]{1,0:T(8,128)(2,1)S(1)}, u32[]{:S(2)}, u32[]{:S(2)}) collective-permute-start(bf16[512,256]{1,0:T(8,128)(2,1)S(1)} %add.325), channel_id=1, source_target_pairs={{2,4},{4,2},{3,5},{5,3},{10,12},{12,10},{11,13},{13,11},{18,20},{2... | collective-permute-start | bytes 786440 | tf_op jit(solution)/shard_map/ppermute | solution.py:329
  312.6 9.9 %collective-permute-start.38 = (bf16[512,256]{1,0:T(8,128)(2,1)S(1)}, bf16[512,256]{1,0:T(8,128)(2,1)S(1)}, u32[]{:S(2)}, u32[]{:S(2)}) collective-permute-start(bf16[512,256]{1,0:T(8,128)(2,1)S(1)} %add_select_fusion.1), channel_id=1, source_target_pairs={{0,2},{2,0},{4,6},{6,4},{1,3},{3,1},{5,7},{7,5},{8,10},{10,8},{12,... | collective-permute-start | bytes 786440 | tf_op jit(solution)/shard_map/ppermute | solution.py:333
  317.4 12.1 %collective-permute-start.40 = (bf16[512,256]{1,0:T(8,128)(2,1)S(1)}, bf16[512,256]{1,0:T(8,128)(2,1)S(1)}, u32[]{:S(2)}, u32[]{:S(2)}) collective-permute-start(bf16[512,256]{1,0:T(8,128)(2,1)S(1)} %add_select_fusion), channel_id=1, source_target_pairs={{0,2},{2,0},{4,6},{6,4},{1,3},{3,1},{5,7},{7,5},{8,10},{10,8},{12,... | collective-permute-start | bytes 786440 | tf_op jit(solution)/shard_map/ppermute | solution.py:333
  320.9 1.6 collective-permute-start.41
  321.5 7.8 %collective-permute-start.43 = (bf16[512,256]{1,0:T(8,128)(2,1)S(1)}, bf16[512,256]{1,0:T(8,128)(2,1)S(1)}, u32[]{:S(2)}, u32[]{:S(2)}) collective-permute-start(bf16[512,256]{1,0:T(8,128)(2,1)S(1)} %add.333), channel_id=1, source_target_pairs={{2,4},{4,2},{3,5},{5,3},{10,12},{12,10},{11,13},{13,11},{18,20},{2... | collective-permute-start | bytes 786440 | tf_op jit(solution)/shard_map/ppermute | solution.py:329
  322.7 23.8 %collective-permute-start.42 = (bf16[512,256]{1,0:T(8,128)(2,1)S(1)}, bf16[512,256]{1,0:T(8,128)(2,1)S(1)}, u32[]{:S(2)}, u32[]{:S(2)}) collective-permute-start(bf16[512,256]{1,0:T(8,128)(2,1)S(1)} %add.336), channel_id=1, source_target_pairs={{0,2},{2,0},{4,6},{6,4},{1,3},{3,1},{5,7},{7,5},{8,10},{10,8},{12,... | collective-permute-start | bytes 786440 | tf_op jit(solution)/shard_map/ppermute | solution.py:333
  329.5 17.1 %collective-permute-start.44 = (bf16[512,256]{1,0:T(8,128)(2,1)S(1)}, bf16[512,256]{1,0:T(8,128)(2,1)S(1)}, u32[]{:S(2)}, u32[]{:S(2)}) collective-permute-start(bf16[512,256]{1,0:T(8,128)(2,1)S(1)} %add.340), channel_id=1, source_target_pairs={{0,2},{2,0},{4,6},{6,4},{1,3},{3,1},{5,7},{7,5},{8,10},{10,8},{12,... | collective-permute-start | bytes 786440 | tf_op jit(solution)/shard_map/ppermute | solution.py:333
  334.7 1.6 collective-permute-start.45
  335.3 7.7 %collective-permute-start.47 = (bf16[512,256]{1,0:T(8,128)(2,1)S(1)}, bf16[512,256]{1,0:T(8,128)(2,1)S(1)}, u32[]{:S(2)}, u32[]{:S(2)}) collective-permute-start(bf16[512,256]{1,0:T(8,128)(2,1)S(1)} %add.341), channel_id=1, source_target_pairs={{2,4},{4,2},{3,5},{5,3},{10,12},{12,10},{11,13},{13,11},{18,20},{2... | collective-permute-start | bytes 786440 | tf_op jit(solution)/shard_map/ppermute | solution.py:329
  336.4 11.0 %collective-permute-start.46 = (bf16[512,256]{1,0:T(8,128)(2,1)S(1)}, bf16[512,256]{1,0:T(8,128)(2,1)S(1)}, u32[]{:S(2)}, u32[]{:S(2)}) collective-permute-start(bf16[512,256]{1,0:T(8,128)(2,1)S(1)} %add.344), channel_id=1, source_target_pairs={{0,2},{2,0},{4,6},{6,4},{1,3},{3,1},{5,7},{7,5},{8,10},{10,8},{12,... | collective-permute-start | bytes 786440 | tf_op jit(solution)/shard_map/ppermute | solution.py:333
  343.2 7.6 %collective-permute-start.48 = (bf16[512,256]{1,0:T(8,128)(2,1)S(1)}, bf16[512,256]{1,0:T(8,128)(2,1)S(1)}, u32[]{:S(2)}, u32[]{:S(2)}) collective-permute-start(bf16[512,256]{1,0:T(8,128)(2,1)S(1)} %add.347), channel_id=1, source_target_pairs={{0,2},{2,0},{4,6},{6,4},{1,3},{3,1},{5,7},{7,5},{8,10},{10,8},{12,... | collective-permute-start | bytes 786440 | tf_op jit(solution)/shard_map/ppermute | solution.py:333
  (12 other events, 215.4 us)

commit v2 on v1

--- a/solution.py
+++ b/solution.py
@@ -327,7 +327,7 @@
             both = own[mid] + outer_got[mid]
             send, both, outer_got[mid] = lax.optimization_barrier((send, both, outer_got[mid]))
             middle_got.append(lax.ppermute(both, "row", middle))
-        if len(own) < CHUNKS and step >= len(own) - 1:
+        if len(own) < CHUNKS and step >= len(own) - 3:
             x, send = lax.optimization_barrier((x, send))
             own.extend(group(len(own), x))
         outer_got.append(lax.ppermute(send, "row", ends))

time: 353 us -> 348 us (0.986)
  transfers between devices with their start and end apart: 50 -> 50, of which waited for: 22 -> 24; matrix products, arithmetic and copies ran while one was open for 3% -> 3% of each run, Pallas kernels for 8% -> 8%
where the time goes in v2:
time: 348 us
  waiting for transfers between devices  115 us (33%)
  starting transfers between devices  82.1 us (24%)
  Pallas kernels  78.2 us (22%)
  blocking collectives  41.7 us (12%)
  other arithmetic  11.7 us (3%)
  local copies, waits for them, and re-layouts  11 us (3%)
  matrix products  6.24 us (2%)
    ppermute x16, starting transfers between devices, solve_and_sum_rows(): outer_got.append(lax.ppermute(send, 'row', ends))  49.9 us
    all_to_all x1, blocking collectives, per_device(): lax.all_to_all(wanted.reshape(devices * per_owner, width), ALL, 0, 0, til...  41.7 us
    pallas_call x7, Pallas kernels, dot_t(): pl.pallas_call(kernel, grid=(count,), in_specs=[pl.BlockSpec((k, tile), l...  25.9 us
    pallas_call x2, Pallas kernels, matmul_streamed(): pl.pallas_call(kernel, in_specs=[pl.BlockSpec(memory_space=pltpu.HBM)] *...  25.5 us
    all_to_all x1, waiting for transfers between devices, per_device(): arrived = lax.all_to_all(packed, ALL, 0, 0, tiled=True)  24.6 us
    ppermute x4, waiting for transfers between devices, swap_leaves(): lax.ppermute(h.astype(BF16), 'leaf', [(i, i ^ order[step]) for i in range...  23.8 us
    ppermute x3, waiting for transfers between devices, solve_and_scatter(): lax.ppermute(summed[d], 'row', [(j, (j + d) % depth) for j in range(depth)])  23.1 us
    ppermute x3, waiting for transfers between devices, gather_and_solve(): lax.ppermute(own, 'row', [(i, (i + d) % depth) for i in range(depth)])  16.4 us
  transfers between devices with their start and end apart: 50, of which 24 were waited for; matrix products, arithmetic and copies ran while one was open for 3% of the time, Pallas kernels for 8%

profile of v2, /device:TPU:0, one launch (start us, length us, event | category | flops | bytes accessed | tf_op | source)
XLA Modules:
  0.0 347.6 jit_solution(10334522785520251927)
XLA Ops:
  0.6 16.3 %shard_map.77 = bf16[3072,256]{1,0:T(8,128)(2,1)S(1)} custom-call(bf16[3072,6144]{1,0:T(8,128)(2,1)} %bitcast.104, bf16[6144,256]{1,0:T(8,128)(2,1)} %bitcast.117), custom_call_target="tpu_custom_call" | custom-call | flops 9663676416 | bytes 37748736 | tf_op jit(solution)/shard_map/pallas_call | solution.py:90
  18.9 2.2 convert_reduce_fusion
  21.2 1.5 add_convert_fusion.x_ref
  22.7 9.2 %shard_map.78 = bf16[3072,256]{1,0:T(8,128)(2,1)S(1)} custom-call(bf16[3072,3072]{1,0:T(8,128)(2,1)} %bitcast.112, bf16[3072,256]{1,0:T(8,128)(2,1)} %add_convert_fusion.x_ref), custom_call_target="tpu_custom_call" | custom-call | flops 4831838208 | bytes 18874368 | tf_op jit(solution)/shard_map/pallas_call | solution.py:90
  31.9 3.4 fusion.4
  36.7 7.0 %all-to-all-start = ((bf16[32,96,256]{2,1,0:T(8,128)(2,1)}), bf16[32,96,256]{2,1,0:T(8,128)(2,1)S(1)}, u32[]{:S(2)}, u32[]{:S(2)}) async-start(bf16[32,96,256]{2,1,0:T(8,128)(2,1)} %bitcast.19), calls=%async_computation | async-start | bytes 3145728 | tf_op jit(solution)/shard_map/all_to_all | solution.py:378
  43.6 1.7 select_reduce_fusion
  45.6 2.7 collective-permute-start.3
  49.3 6.6 %collective-permute-done.3 = s32[32,96]{1,0:T(8,128)S(1)} collective-permute-done((s32[32,96]{1,0:T(8,128)S(1)}, s32[32,96]{1,0:T(8,128)S(1)}, u32[]{:S(2)}, u32[]{:S(2)}) %collective-permute-start.3) | collective-permute-done | bytes 12320 | tf_op jit(solution)/shard_map/ppermute | solution.py:48
  57.9 24.6 %all-to-all-done = bf16[32,96,256]{2,1,0:T(8,128)(2,1)S(1)} async-done(((bf16[32,96,256]{2,1,0:T(8,128)(2,1)}), bf16[32,96,256]{2,1,0:T(8,128)(2,1)S(1)}, u32[]{:S(2)}, u32[]{:S(2)}) %all-to-all-start) | async-done | bytes 1572896 | tf_op jit(solution)/shard_map/all_to_all | solution.py:378
  83.5 9.6 %collective-permute-done.8.refs_2_ = bf16[512,256]{1,0:T(8,128)(2,1)S(1)} collective-permute-done((bf16[512,256]{1,0:T(8,128)(2,1)S(1)}, bf16[512,256]{1,0:T(8,128)(2,1)S(1)}, u32[]{:S(2)}, u32[]{:S(2)}) %collective-permute-start.8) | collective-permute-done | bytes 262176 | tf_op jit(solution)/shard_map/ppermute | solution.py:179
  94.6 6.1 %shard_map.79.refs_4_ = f32[2048,256]{1,0:T(8,128)S(1)} custom-call(s32[4]{0:T(128)S(1)} %pad_add_fusion.3.chunks_ref, bf16[2048,4096]{1,0:T(8,128)(2,1)} %a_ref.5, bf16[512,256]{1,0:T(8,128)(2,1)S(1)} %fusion.10.refs_0_, bf16[512,256]{1,0:T(8,128)(2,1)S(1)} %collective-permute-done.7.refs_1_, bf16[512,256]{1,0:T(8,128)(2,1)S(1)} %collective-permute-done.8.refs_2_, ...), custom_call_target="tpu_custom_call" | custom-call | flops 2147483648 | bytes 16777216 | tf_op jit(solution)/shard_map/pallas_call | solution.py:154
  100.7 5.6 %collective-permute-done.5.refs_0_ = bf16[512,256]{1,0:T(8,128)(2,1)S(1)} collective-permute-done((bf16[512,256]{1,0:T(8,128)(2,1)S(1)}, bf16[512,256]{1,0:T(8,128)(2,1)S(1)}, u32[]{:S(2)}, u32[]{:S(2)}) %collective-permute-start.5) | collective-permute-done | bytes 262176 | tf_op jit(solution)/shard_map/ppermute | solution.py:179
  109.6 5.8 %copy-done = bf16[2048,4096]{1,0:T(8,128)(2,1)S(1)} copy-done((bf16[2048,4096]{1,0:T(8,128)(2,1)S(1)}, bf16[2048,4096]{1,0:T(8,128)(2,1)}, u32[]{:S(2)}) %copy-start) | copy-done | bytes 16777240
  115.4 4.0 %shard_map.80 = f32[2048,256]{1,0:T(8,128)S(1)} custom-call(s32[4]{0:T(128)S(1)} %pad_add_fusion.2.chunks_ref, bf16[2048,4096]{1,0:T(8,128)(2,1)S(1)} %copy-done, bf16[512,256]{1,0:T(8,128)(2,1)S(1)} %collective-permute-done.5.refs_0_, bf16[512,256]{1,0:T(8,128)(2,1)S(1)} %collective-permute-done.10.refs_1_, ...), custom_call_target="tpu_custom_call" | custom-call | flops 2147483648 | tf_op jit(solution)/shard_map/pallas_call | solution.py:127
  121.3 12.3 %collective-permute-done.12 = bf16[1024,256]{1,0:T(8,128)(2,1)S(1)} collective-permute-done((bf16[1024,256]{1,0:T(8,128)(2,1)S(1)}, bf16[1024,256]{1,0:T(8,128)(2,1)S(1)}, u32[]{:S(2)}, u32[]{:S(2)}) %collective-permute-start.12) | collective-permute-done | bytes 524320 | tf_op jit(solution)/shard_map/ppermute | solution.py:38
  137.0 10.3 %collective-permute-done.13 = bf16[1024,256]{1,0:T(8,128)(2,1)S(1)} collective-permute-done((bf16[1024,256]{1,0:T(8,128)(2,1)S(1)}, bf16[1024,256]{1,0:T(8,128)(2,1)S(1)}, u32[]{:S(2)}, u32[]{:S(2)}) %collective-permute-start.13) | collective-permute-done | bytes 524320 | tf_op jit(solution)/shard_map/ppermute | solution.py:38
  148.6 7.2 %shard_map.81 = bf16[8,512,256]{2,1,0:T(8,128)(2,1)S(1)} custom-call(s32[2]{0:T(128)S(1)} %pad_add_fusion.1.which_ref, bf16[2048,4096]{1,0:T(8,128)(2,1)S(1)} %bitcast.101, bf16[2048,256]{1,0:T(8,128)(2,1)S(1)} %pad_maximum_fusion.x_ref), custom_call_target="tpu_custom_call" | custom-call | flops 4294967296 | tf_op jit(solution)/shard_map/pallas_call | solution.py:216
  155.9 2.6 collective-permute-done.16
  158.8 6.0 %collective-permute-start.19 = (bf16[512,256]{1,0:T(8,128)(2,1)S(1)}, bf16[512,256]{1,0:T(8,128)(2,1)S(1)}, u32[]{:S(2)}, u32[]{:S(2)}) collective-permute-start(bf16[512,256]{1,0:T(8,128)(2,1)S(1)} %get-tuple-element.131), channel_id=1, source_target_pairs={{0,6},{2,0},{4,2},{6,4},{1,7},{3,1},{5,3},{7,5},{8,14},{10,8},{12,... | collective-permute-start | bytes 786440 | tf_op jit(solution)/shard_map/ppermute | solution.py:295
  165.4 6.1 %collective-permute-done.19 = bf16[512,256]{1,0:T(8,128)(2,1)S(1)} collective-permute-done((bf16[512,256]{1,0:T(8,128)(2,1)S(1)}, bf16[512,256]{1,0:T(8,128)(2,1)S(1)}, u32[]{:S(2)}, u32[]{:S(2)}) %collective-permute-start.19) | collective-permute-done | bytes 262176 | tf_op jit(solution)/shard_map/ppermute | solution.py:295
  171.5 17.0 %collective-permute-done.18 = bf16[512,256]{1,0:T(8,128)(2,1)S(1)} collective-permute-done((bf16[512,256]{1,0:T(8,128)(2,1)S(1)}, bf16[512,256]{1,0:T(8,128)(2,1)S(1)}, u32[]{:S(2)}, u32[]{:S(2)}) %collective-permute-start.18) | collective-permute-done | bytes 262176 | tf_op jit(solution)/shard_map/ppermute | solution.py:295
  189.4 41.7 %all_to_all.18 = bf16[32,96,256]{2,1,0:T(8,128)(2,1)S(1)} all-to-all(bf16[32,96,256]{2,1,0:T(8,128)(2,1)S(1)} %bitcast.116), channel_id=1, replica_groups=mesh['leaf'=4,'row'=4,'col'=2] {'leaf','row','col'}, dimensions={0} | all-to-all | bytes 3145728 | tf_op jit(solution)/shard_map/all_to_all | solution.py:391
  231.3 1.9 fusion.5
  233.2 9.5 %shard_map.82 = bf16[3072,256]{1,0:T(8,128)(2,1)S(1)} custom-call(bf16[3072,3072]{1,0:T(8,128)(2,1)} %bitcast.113, bf16[3072,256]{1,0:T(8,128)(2,1)S(1)} %bitcast.102), custom_call_target="tpu_custom_call" | custom-call | flops 4831838208 | bytes 18874368 | tf_op jit(solution)/shard_map/pallas_call | solution.py:268
  242.8 3.4 collective-permute-done.20
  246.8 2.9 shard_map.83
  249.8 2.9 shard_map.84
  252.7 2.1 collective-permute-start.25
  254.8 4.0 %shard_map.85 = (bf16[512,256]{1,0:T(8,128)(2,1)S(1)}, bf16[512,256]{1,0:T(8,128)(2,1)S(1)}) custom-call(bf16[3072,6144]{1,0:T(8,128)(2,1)} %bitcast.107, bf16[3072,256]{1,0:T(8,128)(2,1)S(1)} %subtract_convert_fusion.x_ref), custom_call_target="tpu_custom_call" | custom-call | flops 1610612736 | bytes 6291456 | tf_op jit(solution)/shard_map/pallas_call | solution.py:242
  260.9 3.6 %collective-permute-done.25 = bf16[512,256]{1,0:T(8,128)(2,1)S(1)} collective-permute-done((bf16[512,256]{1,0:T(8,128)(2,1)S(1)}, bf16[512,256]{1,0:T(8,128)(2,1)S(1)}, u32[]{:S(2)}, u32[]{:S(2)}) %collective-permute-start.25) | collective-permute-done | bytes 262176 | tf_op jit(solution)/shard_map/ppermute | solution.py:333
  266.5 4.0 %shard_map.86 = (bf16[512,256]{1,0:T(8,128)(2,1)S(1)}, bf16[512,256]{1,0:T(8,128)(2,1)S(1)}) custom-call(bf16[3072,6144]{1,0:T(8,128)(2,1)} %bitcast.108, bf16[3072,256]{1,0:T(8,128)(2,1)S(1)} %subtract_convert_fusion.x_ref), custom_call_target="tpu_custom_call" | custom-call | flops 1610612736 | bytes 6291456 | tf_op jit(solution)/shard_map/pallas_call | solution.py:242
  270.6 4.0 %shard_map.87 = (bf16[512,256]{1,0:T(8,128)(2,1)S(1)}, bf16[512,256]{1,0:T(8,128)(2,1)S(1)}) custom-call(bf16[3072,6144]{1,0:T(8,128)(2,1)} %bitcast.109, bf16[3072,256]{1,0:T(8,128)(2,1)S(1)} %subtract_convert_fusion.x_ref), custom_call_target="tpu_custom_call" | custom-call | flops 1610612736 | bytes 6291456 | tf_op jit(solution)/shard_map/pallas_call | solution.py:242
  278.4 4.0 %shard_map.88 = (bf16[512,256]{1,0:T(8,128)(2,1)S(1)}, bf16[512,256]{1,0:T(8,128)(2,1)S(1)}) custom-call(bf16[3072,6144]{1,0:T(8,128)(2,1)} %bitcast.110, bf16[3072,256]{1,0:T(8,128)(2,1)S(1)} %subtract_convert_fusion.x_ref), custom_call_target="tpu_custom_call" | custom-call | flops 1610612736 | bytes 6291456 | tf_op jit(solution)/shard_map/pallas_call | solution.py:242
  282.4 1.6 collective-permute-done.24
  284.5 4.5 %collective-permute-start.30 = (bf16[512,256]{1,0:T(8,128)(2,1)S(1)}, bf16[512,256]{1,0:T(8,128)(2,1)S(1)}, u32[]{:S(2)}, u32[]{:S(2)}) collective-permute-start(bf16[512,256]{1,0:T(8,128)(2,1)S(1)} %add_select_fusion.5), channel_id=1, source_target_pairs={{0,2},{2,0},{4,6},{6,4},{1,3},{3,1},{5,7},{7,5},{8,10},{10,8},{12,... | collective-permute-start | bytes 786440 | tf_op jit(solution)/shard_map/ppermute | solution.py:333
  289.2 2.7 collective-permute-start.32
  293.7 4.0 %shard_map.89 = (bf16[512,256]{1,0:T(8,128)(2,1)S(1)}, bf16[512,256]{1,0:T(8,128)(2,1)S(1)}) custom-call(bf16[3072,6144]{1,0:T(8,128)(2,1)} %bitcast.111, bf16[3072,256]{1,0:T(8,128)(2,1)S(1)} %subtract_convert_fusion.x_ref), custom_call_target="tpu_custom_call" | custom-call | flops 1610612736 | bytes 6291456 | tf_op jit(solution)/shard_map/pallas_call | solution.py:242
  297.9 4.8 %collective-permute-start.34 = (bf16[512,256]{1,0:T(8,128)(2,1)S(1)}, bf16[512,256]{1,0:T(8,128)(2,1)S(1)}, u32[]{:S(2)}, u32[]{:S(2)}) collective-permute-start(bf16[512,256]{1,0:T(8,128)(2,1)S(1)} %add_select_fusion.3), channel_id=1, source_target_pairs={{0,2},{2,0},{4,6},{6,4},{1,3},{3,1},{5,7},{7,5},{8,10},{10,8},{12,... | collective-permute-start | bytes 786440 | tf_op jit(solution)/shard_map/ppermute | solution.py:333
  302.8 2.7 collective-permute-start.36
  308.7 6.4 %collective-permute-start.38 = (bf16[512,256]{1,0:T(8,128)(2,1)S(1)}, bf16[512,256]{1,0:T(8,128)(2,1)S(1)}, u32[]{:S(2)}, u32[]{:S(2)}) collective-permute-start(bf16[512,256]{1,0:T(8,128)(2,1)S(1)} %add_select_fusion.1), channel_id=1, source_target_pairs={{0,2},{2,0},{4,6},{6,4},{1,3},{3,1},{5,7},{7,5},{8,10},{10,8},{12,... | collective-permute-start | bytes 786440 | tf_op jit(solution)/shard_map/ppermute | solution.py:333
  315.3 2.7 collective-permute-start.40
  320.2 6.6 %collective-permute-start.42 = (bf16[512,256]{1,0:T(8,128)(2,1)S(1)}, bf16[512,256]{1,0:T(8,128)(2,1)S(1)}, u32[]{:S(2)}, u32[]{:S(2)}) collective-permute-start(bf16[512,256]{1,0:T(8,128)(2,1)S(1)} %add.336), channel_id=1, source_target_pairs={{0,2},{2,0},{4,6},{6,4},{1,3},{3,1},{5,7},{7,5},{8,10},{10,8},{12,... | collective-permute-start | bytes 786440 | tf_op jit(solution)/shard_map/ppermute | solution.py:333
  327.0 3.1 collective-permute-start.44
  331.8 6.7 %collective-permute-start.46 = (bf16[512,256]{1,0:T(8,128)(2,1)S(1)}, bf16[512,256]{1,0:T(8,128)(2,1)S(1)}, u32[]{:S(2)}, u32[]{:S(2)}) collective-permute-start(bf16[512,256]{1,0:T(8,128)(2,1)S(1)} %add.344), channel_id=1, source_target_pairs={{0,2},{2,0},{4,6},{6,4},{1,3},{3,1},{5,7},{7,5},{8,10},{10,8},{12,... | collective-permute-start | bytes 786440 | tf_op jit(solution)/shard_map/ppermute | solution.py:333
  338.6 2.8 collective-permute-start.48
  343.0 2.8 collective-permute-done.48
  345.9 1.7 copy-done.2
  (165 shorter events, 41.0 us)
Async XLA Ops:
  17.0 4.2 %collective-permute-start = (bf16[3072,256]{1,0:T(8,128)(2,1)S(1)}, bf16[3072,256]{1,0:T(8,128)(2,1)S(1)}, u32[]{:S(2)}, u32[]{:S(2)}) collective-permute-start(bf16[3072,256]{1,0:T(8,128)(2,1)S(1)} %shard_map.77), channel_id=1, source_target_pairs={{0,1},{1,0},{2,3},{3,2},{4,5},{5,4},{6,7},{7,6},{8,9},{9,8},{10,11... | collective-permute-start | bytes 4718600 | tf_op jit(solution)/shard_map/ppermute | solution.py:27
  36.7 45.8 %all-to-all-start = ((bf16[32,96,256]{2,1,0:T(8,128)(2,1)}), bf16[32,96,256]{2,1,0:T(8,128)(2,1)S(1)}, u32[]{:S(2)}, u32[]{:S(2)}) async-start(bf16[32,96,256]{2,1,0:T(8,128)(2,1)} %bitcast.19), calls=%async_computation | async-start | bytes 3145728 | tf_op jit(solution)/shard_map/all_to_all | solution.py:378
  45.6 10.3 %collective-permute-start.3 = (s32[32,96]{1,0:T(8,128)S(1)}, s32[32,96]{1,0:T(8,128)S(1)}, u32[]{:S(2)}, u32[]{:S(2)}) collective-permute-start(s32[32,96]{1,0:T(8,128)S(1)} %reshape.183), channel_id=1, source_target_pairs={{0,24},{8,16},{16,8},{24,0},{1,25},{9,17},{17,9},{25,1},{2,26},{10... | collective-permute-start | bytes 36872 | tf_op jit(solution)/shard_map/ppermute | solution.py:48
  48.3 7.6 %collective-permute-start.2 = (s32[32,96]{1,0:T(8,128)S(1)}, s32[32,96]{1,0:T(8,128)S(1)}, u32[]{:S(2)}, u32[]{:S(2)}) collective-permute-start(s32[32,96]{1,0:T(8,128)S(1)} %reshape.183), channel_id=1, source_target_pairs={{0,16},{8,24},{16,0},{24,8},{1,17},{9,25},{17,1},{25,9},{2,18},{10... | collective-permute-start | bytes 36872 | tf_op jit(solution)/shard_map/ppermute | solution.py:48
  48.9 7.0 %collective-permute-start.1 = (s32[32,96]{1,0:T(8,128)S(1)}, s32[32,96]{1,0:T(8,128)S(1)}, u32[]{:S(2)}, u32[]{:S(2)}) collective-permute-start(s32[32,96]{1,0:T(8,128)S(1)} %reshape.183), channel_id=1, source_target_pairs={{0,8},{8,0},{16,24},{24,16},{1,9},{9,1},{17,25},{25,17},{2,10},{10... | collective-permute-start | bytes 36872 | tf_op jit(solution)/shard_map/ppermute | solution.py:48
  83.3 9.7 %collective-permute-start.8 = (bf16[512,256]{1,0:T(8,128)(2,1)S(1)}, bf16[512,256]{1,0:T(8,128)(2,1)S(1)}, u32[]{:S(2)}, u32[]{:S(2)}) collective-permute-start(bf16[512,256]{1,0:T(8,128)(2,1)S(1)} %fusion.10.refs_0_), channel_id=1, source_target_pairs={{0,2},{2,4},{4,6},{6,0},{1,3},{3,5},{5,7},{7,1},{8,10},{10,12},{12... | collective-permute-start | bytes 786440 | tf_op jit(solution)/shard_map/ppermute | solution.py:179
  83.4 10.6 %collective-permute-start.7 = (bf16[512,256]{1,0:T(8,128)(2,1)S(1)}, bf16[512,256]{1,0:T(8,128)(2,1)S(1)}, u32[]{:S(2)}, u32[]{:S(2)}) collective-permute-start(bf16[512,256]{1,0:T(8,128)(2,1)S(1)} %fusion.10.refs_0_), channel_id=1, source_target_pairs={{0,1},{1,0},{2,3},{3,2},{4,5},{5,4},{6,7},{7,6},{8,9},{9,8},{10,11... | collective-permute-start | bytes 786440 | tf_op jit(solution)/shard_map/ppermute | solution.py:192
  93.1 13.3 %collective-permute-start.5 = (bf16[512,256]{1,0:T(8,128)(2,1)S(1)}, bf16[512,256]{1,0:T(8,128)(2,1)S(1)}, u32[]{:S(2)}, u32[]{:S(2)}) collective-permute-start(bf16[512,256]{1,0:T(8,128)(2,1)S(1)} %fusion.10.refs_0_), channel_id=1, source_target_pairs={{0,4},{2,6},{4,0},{6,2},{1,5},{3,7},{5,1},{7,3},{8,12},{10,14},{12... | collective-permute-start | bytes 786440 | tf_op jit(solution)/shard_map/ppermute | solution.py:179
  93.1 14.4 %collective-permute-start.6 = (bf16[512,256]{1,0:T(8,128)(2,1)S(1)}, bf16[512,256]{1,0:T(8,128)(2,1)}, u32[]{:S(2)}, u32[]{:S(2)}) collective-permute-start(bf16[512,256]{1,0:T(8,128)(2,1)S(1)} %fusion.10.refs_0_), channel_id=1, source_target_pairs={{0,6},{2,0},{4,2},{6,4},{1,7},{3,1},{5,3},{7,5},{8,14},{10,8},{12,... | collective-permute-start | bytes 786440 | tf_op jit(solution)/shard_map/ppermute | solution.py:179
  107.5 1.9 collective-permute-start.10
  107.5 2.1 collective-permute-start.11
  119.5 14.1 %collective-permute-start.12 = (bf16[1024,256]{1,0:T(8,128)(2,1)S(1)}, bf16[1024,256]{1,0:T(8,128)(2,1)S(1)}, u32[]{:S(2)}, u32[]{:S(2)}) collective-permute-start(bf16[1024,256]{1,0:T(8,128)(2,1)S(1)} %get-tuple-element.128), channel_id=1, source_target_pairs={{0,8},{8,0},{16,24},{24,16},{1,9},{9,1},{17,25},{25,17},{2,10},{10... | collective-permute-start | bytes 1572872 | tf_op jit(solution)/shard_map/ppermute | solution.py:38
  120.3 13.7 %collective-permute-start.14 = (bf16[1024,256]{1,0:T(8,128)(2,1)S(1)}, bf16[1024,256]{1,0:T(8,128)(2,1)S(1)}, u32[]{:S(2)}, u32[]{:S(2)}) collective-permute-start(bf16[1024,256]{1,0:T(8,128)(2,1)S(1)} %get-tuple-element.129), channel_id=1, source_target_pairs={{0,16},{8,24},{16,0},{24,8},{1,17},{9,25},{17,1},{25,9},{2,18},{10... | collective-permute-start | bytes 1572872 | tf_op jit(solution)/shard_map/ppermute | solution.py:38
  134.3 12.9 %collective-permute-start.13 = (bf16[1024,256]{1,0:T(8,128)(2,1)S(1)}, bf16[1024,256]{1,0:T(8,128)(2,1)S(1)}, u32[]{:S(2)}, u32[]{:S(2)}) collective-permute-start(bf16[1024,256]{1,0:T(8,128)(2,1)S(1)} %get-tuple-element.126), channel_id=1, source_target_pairs={{0,16},{8,24},{16,0},{24,8},{1,17},{9,25},{17,1},{25,9},{2,18},{10... | collective-permute-start | bytes 1572872 | tf_op jit(solution)/shard_map/ppermute | solution.py:38
  135.4 12.7 %collective-permute-start.15 = (bf16[1024,256]{1,0:T(8,128)(2,1)S(1)}, bf16[1024,256]{1,0:T(8,128)(2,1)S(1)}, u32[]{:S(2)}, u32[]{:S(2)}) collective-permute-start(bf16[1024,256]{1,0:T(8,128)(2,1)S(1)} %get-tuple-element.127), channel_id=1, source_target_pairs={{0,8},{8,0},{16,24},{24,16},{1,9},{9,1},{17,25},{25,17},{2,10},{10... | collective-permute-start | bytes 1572872 | tf_op jit(solution)/shard_map/ppermute | solution.py:38
  155.8 2.7 collective-permute-start.16
  158.8 12.8 %collective-permute-start.19 = (bf16[512,256]{1,0:T(8,128)(2,1)S(1)}, bf16[512,256]{1,0:T(8,128)(2,1)S(1)}, u32[]{:S(2)}, u32[]{:S(2)}) collective-permute-start(bf16[512,256]{1,0:T(8,128)(2,1)S(1)} %get-tuple-element.131), channel_id=1, source_target_pairs={{0,6},{2,0},{4,2},{6,4},{1,7},{3,1},{5,3},{7,5},{8,14},{10,8},{12,... | collective-permute-start | bytes 786440 | tf_op jit(solution)/shard_map/ppermute | solution.py:295
  164.8 23.7 %collective-permute-start.18 = (bf16[512,256]{1,0:T(8,128)(2,1)S(1)}, bf16[512,256]{1,0:T(8,128)(2,1)S(1)}, u32[]{:S(2)}, u32[]{:S(2)}) collective-permute-start(bf16[512,256]{1,0:T(8,128)(2,1)S(1)} %get-tuple-element.132), channel_id=1, source_target_pairs={{0,4},{2,6},{4,0},{6,2},{1,5},{3,7},{5,1},{7,3},{8,12},{10,14},{12... | collective-permute-start | bytes 786440 | tf_op jit(solution)/shard_map/ppermute | solution.py:295
  165.3 23.2 %collective-permute-start.17 = (bf16[512,256]{1,0:T(8,128)(2,1)S(1)}, bf16[512,256]{1,0:T(8,128)(2,1)S(1)}, u32[]{:S(2)}, u32[]{:S(2)}) collective-permute-start(bf16[512,256]{1,0:T(8,128)(2,1)S(1)} %get-tuple-element.130), channel_id=1, source_target_pairs={{0,2},{2,4},{4,6},{6,0},{1,3},{3,5},{5,7},{7,1},{8,10},{10,12},{12... | collective-permute-start | bytes 786440 | tf_op jit(solution)/shard_map/ppermute | solution.py:295
  242.7 3.5 %collective-permute-start.20 = (bf16[3072,256]{1,0:T(8,128)(2,1)S(1)}, bf16[3072,256]{1,0:T(8,128)(2,1)S(1)}, u32[]{:S(2)}, u32[]{:S(2)}) collective-permute-start(bf16[3072,256]{1,0:T(8,128)(2,1)S(1)} %shard_map.82), channel_id=1, source_target_pairs={{0,1},{1,0},{2,3},{3,2},{4,5},{5,4},{6,7},{7,6},{8,9},{9,8},{10,11... | collective-permute-start | bytes 4718600 | tf_op jit(solution)/shard_map/ppermute | solution.py:27
  249.7 9.2 %collective-permute-start.21 = (bf16[512,256]{1,0:T(8,128)(2,1)S(1)}, bf16[512,256]{1,0:T(8,128)(2,1)S(1)}, u32[]{:S(2)}, u32[]{:S(2)}) collective-permute-start(bf16[512,256]{1,0:T(8,128)(2,1)S(1)} %shard_map.83), channel_id=1, source_target_pairs={{0,2},{2,0},{4,6},{6,4},{1,3},{3,1},{5,7},{7,5},{8,10},{10,8},{12,... | collective-permute-start | bytes 786440 | tf_op jit(solution)/shard_map/ppermute | solution.py:333
  252.7 11.8 %collective-permute-start.25 = (bf16[512,256]{1,0:T(8,128)(2,1)S(1)}, bf16[512,256]{1,0:T(8,128)(2,1)S(1)}, u32[]{:S(2)}, u32[]{:S(2)}) collective-permute-start(bf16[512,256]{1,0:T(8,128)(2,1)S(1)} %shard_map.84), channel_id=1, source_target_pairs={{0,2},{2,0},{4,6},{6,4},{1,3},{3,1},{5,7},{7,5},{8,10},{10,8},{12,... | collective-permute-start | bytes 786440 | tf_op jit(solution)/shard_map/ppermute | solution.py:333
  259.0 15.6 %collective-permute-start.22 = (bf16[512,256]{1,0:T(8,128)(2,1)S(1)}, bf16[512,256]{1,0:T(8,128)(2,1)S(1)}, u32[]{:S(2)}, u32[]{:S(2)}) collective-permute-start(bf16[512,256]{1,0:T(8,128)(2,1)S(1)} %add.301), channel_id=1, source_target_pairs={{2,4},{4,2},{3,5},{5,3},{10,12},{12,10},{11,13},{13,11},{18,20},{2... | collective-permute-start | bytes 786440 | tf_op jit(solution)/shard_map/ppermute | solution.py:329
  259.7 15.0 %collective-permute-start.23 = (bf16[512,256]{1,0:T(8,128)(2,1)S(1)}, bf16[512,256]{1,0:T(8,128)(2,1)S(1)}, u32[]{:S(2)}, u32[]{:S(2)}) collective-permute-start(bf16[512,256]{1,0:T(8,128)(2,1)S(1)} %get-tuple-element.75), channel_id=1, source_target_pairs={{0,2},{2,0},{4,6},{6,4},{1,3},{3,1},{5,7},{7,5},{8,10},{10,8},{12,... | collective-permute-start | bytes 786440 | tf_op jit(solution)/shard_map/ppermute | solution.py:333
  264.6 11.0 %collective-permute-start.26 = (bf16[512,256]{1,0:T(8,128)(2,1)S(1)}, bf16[512,256]{1,0:T(8,128)(2,1)S(1)}, u32[]{:S(2)}, u32[]{:S(2)}) collective-permute-start(bf16[512,256]{1,0:T(8,128)(2,1)S(1)} %add.306), channel_id=1, source_target_pairs={{2,4},{4,2},{3,5},{5,3},{10,12},{12,10},{11,13},{13,11},{18,20},{2... | collective-permute-start | bytes 786440 | tf_op jit(solution)/shard_map/ppermute | solution.py:329
  265.3 10.4 %collective-permute-start.27 = (bf16[512,256]{1,0:T(8,128)(2,1)S(1)}, bf16[512,256]{1,0:T(8,128)(2,1)S(1)}, u32[]{:S(2)}, u32[]{:S(2)}) collective-permute-start(bf16[512,256]{1,0:T(8,128)(2,1)S(1)} %get-tuple-element.84), channel_id=1, source_target_pairs={{0,2},{2,0},{4,6},{6,4},{1,3},{3,1},{5,7},{7,5},{8,10},{10,8},{12,... | collective-permute-start | bytes 786440 | tf_op jit(solution)/shard_map/ppermute | solution.py:333
  274.7 9.3 %collective-permute-start.24 = (bf16[512,256]{1,0:T(8,128)(2,1)S(1)}, bf16[512,256]{1,0:T(8,128)(2,1)S(1)}, u32[]{:S(2)}, u32[]{:S(2)}) collective-permute-start(bf16[512,256]{1,0:T(8,128)(2,1)S(1)} %add_select_fusion.7), channel_id=1, source_target_pairs={{0,2},{2,0},{4,6},{6,4},{1,3},{3,1},{5,7},{7,5},{8,10},{10,8},{12,... | collective-permute-start | bytes 786440 | tf_op jit(solution)/shard_map/ppermute | solution.py:333
  275.8 13.3 %collective-permute-start.28 = (bf16[512,256]{1,0:T(8,128)(2,1)S(1)}, bf16[512,256]{1,0:T(8,128)(2,1)S(1)}, u32[]{:S(2)}, u32[]{:S(2)}) collective-permute-start(bf16[512,256]{1,0:T(8,128)(2,1)S(1)} %add_select_fusion.6), channel_id=1, source_target_pairs={{0,2},{2,0},{4,6},{6,4},{1,3},{3,1},{5,7},{7,5},{8,10},{10,8},{12,... | collective-permute-start | bytes 786440 | tf_op jit(solution)/shard_map/ppermute | solution.py:333
  277.0 7.4 %collective-permute-start.29 = (bf16[512,256]{1,0:T(8,128)(2,1)S(1)}, bf16[512,256]{1,0:T(8,128)(2,1)S(1)}, u32[]{:S(2)}, u32[]{:S(2)}) collective-permute-start(bf16[512,256]{1,0:T(8,128)(2,1)S(1)} %add.304), channel_id=1, source_target_pairs={{2,4},{4,2},{3,5},{5,3},{10,12},{12,10},{11,13},{13,11},{18,20},{2... | collective-permute-start | bytes 786440 | tf_op jit(solution)/shard_map/ppermute | solution.py:329
  277.7 11.5 %collective-permute-start.31 = (bf16[512,256]{1,0:T(8,128)(2,1)S(1)}, bf16[512,256]{1,0:T(8,128)(2,1)S(1)}, u32[]{:S(2)}, u32[]{:S(2)}) collective-permute-start(bf16[512,256]{1,0:T(8,128)(2,1)S(1)} %add.309), channel_id=1, source_target_pairs={{2,4},{4,2},{3,5},{5,3},{10,12},{12,10},{11,13},{13,11},{18,20},{2... | collective-permute-start | bytes 786440 | tf_op jit(solution)/shard_map/ppermute | solution.py:329
  284.5 13.2 %collective-permute-start.30 = (bf16[512,256]{1,0:T(8,128)(2,1)S(1)}, bf16[512,256]{1,0:T(8,128)(2,1)S(1)}, u32[]{:S(2)}, u32[]{:S(2)}) collective-permute-start(bf16[512,256]{1,0:T(8,128)(2,1)S(1)} %add_select_fusion.5), channel_id=1, source_target_pairs={{0,2},{2,0},{4,6},{6,4},{1,3},{3,1},{5,7},{7,5},{8,10},{10,8},{12,... | collective-permute-start | bytes 786440 | tf_op jit(solution)/shard_map/ppermute | solution.py:333
  289.2 13.5 %collective-permute-start.32 = (bf16[512,256]{1,0:T(8,128)(2,1)S(1)}, bf16[512,256]{1,0:T(8,128)(2,1)S(1)}, u32[]{:S(2)}, u32[]{:S(2)}) collective-permute-start(bf16[512,256]{1,0:T(8,128)(2,1)S(1)} %add_select_fusion.4), channel_id=1, source_target_pairs={{0,2},{2,0},{4,6},{6,4},{1,3},{3,1},{5,7},{7,5},{8,10},{10,8},{12,... | collective-permute-start | bytes 786440 | tf_op jit(solution)/shard_map/ppermute | solution.py:333
  292.0 5.9 %collective-permute-start.33 = (bf16[512,256]{1,0:T(8,128)(2,1)S(1)}, bf16[512,256]{1,0:T(8,128)(2,1)S(1)}, u32[]{:S(2)}, u32[]{:S(2)}) collective-permute-start(bf16[512,256]{1,0:T(8,128)(2,1)S(1)} %add.313), channel_id=1, source_target_pairs={{2,4},{4,2},{3,5},{5,3},{10,12},{12,10},{11,13},{13,11},{18,20},{2... | collective-permute-start | bytes 786440 | tf_op jit(solution)/shard_map/ppermute | solution.py:329
  292.9 9.9 %collective-permute-start.35 = (bf16[512,256]{1,0:T(8,128)(2,1)S(1)}, bf16[512,256]{1,0:T(8,128)(2,1)S(1)}, u32[]{:S(2)}, u32[]{:S(2)}) collective-permute-start(bf16[512,256]{1,0:T(8,128)(2,1)S(1)} %add.317), channel_id=1, source_target_pairs={{2,4},{4,2},{3,5},{5,3},{10,12},{12,10},{11,13},{13,11},{18,20},{2... | collective-permute-start | bytes 786440 | tf_op jit(solution)/shard_map/ppermute | solution.py:329
  297.9 10.7 %collective-permute-start.34 = (bf16[512,256]{1,0:T(8,128)(2,1)S(1)}, bf16[512,256]{1,0:T(8,128)(2,1)S(1)}, u32[]{:S(2)}, u32[]{:S(2)}) collective-permute-start(bf16[512,256]{1,0:T(8,128)(2,1)S(1)} %add_select_fusion.3), channel_id=1, source_target_pairs={{0,2},{2,0},{4,6},{6,4},{1,3},{3,1},{5,7},{7,5},{8,10},{10,8},{12,... | collective-permute-start | bytes 786440 | tf_op jit(solution)/shard_map/ppermute | solution.py:333
  302.8 12.3 %collective-permute-start.36 = (bf16[512,256]{1,0:T(8,128)(2,1)S(1)}, bf16[512,256]{1,0:T(8,128)(2,1)S(1)}, u32[]{:S(2)}, u32[]{:S(2)}) collective-permute-start(bf16[512,256]{1,0:T(8,128)(2,1)S(1)} %add_select_fusion.2), channel_id=1, source_target_pairs={{0,2},{2,0},{4,6},{6,4},{1,3},{3,1},{5,7},{7,5},{8,10},{10,8},{12,... | collective-permute-start | bytes 786440 | tf_op jit(solution)/shard_map/ppermute | solution.py:333
  305.5 3.2 collective-permute-start.37
  306.2 9.1 %collective-permute-start.39 = (bf16[512,256]{1,0:T(8,128)(2,1)S(1)}, bf16[512,256]{1,0:T(8,128)(2,1)S(1)}, u32[]{:S(2)}, u32[]{:S(2)}) collective-permute-start(bf16[512,256]{1,0:T(8,128)(2,1)S(1)} %add.325), channel_id=1, source_target_pairs={{2,4},{4,2},{3,5},{5,3},{10,12},{12,10},{11,13},{13,11},{18,20},{2... | collective-permute-start | bytes 786440 | tf_op jit(solution)/shard_map/ppermute | solution.py:329
  308.7 11.4 %collective-permute-start.38 = (bf16[512,256]{1,0:T(8,128)(2,1)S(1)}, bf16[512,256]{1,0:T(8,128)(2,1)S(1)}, u32[]{:S(2)}, u32[]{:S(2)}) collective-permute-start(bf16[512,256]{1,0:T(8,128)(2,1)S(1)} %add_select_fusion.1), channel_id=1, source_target_pairs={{0,2},{2,0},{4,6},{6,4},{1,3},{3,1},{5,7},{7,5},{8,10},{10,8},{12,... | collective-permute-start | bytes 786440 | tf_op jit(solution)/shard_map/ppermute | solution.py:333
  315.3 11.6 %collective-permute-start.40 = (bf16[512,256]{1,0:T(8,128)(2,1)S(1)}, bf16[512,256]{1,0:T(8,128)(2,1)S(1)}, u32[]{:S(2)}, u32[]{:S(2)}) collective-permute-start(bf16[512,256]{1,0:T(8,128)(2,1)S(1)} %add_select_fusion), channel_id=1, source_target_pairs={{0,2},{2,0},{4,6},{6,4},{1,3},{3,1},{5,7},{7,5},{8,10},{10,8},{12,... | collective-permute-start | bytes 786440 | tf_op jit(solution)/shard_map/ppermute | solution.py:333
  318.0 1.7 collective-permute-start.41
  318.7 8.2 %collective-permute-start.43 = (bf16[512,256]{1,0:T(8,128)(2,1)S(1)}, bf16[512,256]{1,0:T(8,128)(2,1)S(1)}, u32[]{:S(2)}, u32[]{:S(2)}) collective-permute-start(bf16[512,256]{1,0:T(8,128)(2,1)S(1)} %add.333), channel_id=1, source_target_pairs={{2,4},{4,2},{3,5},{5,3},{10,12},{12,10},{11,13},{13,11},{18,20},{2... | collective-permute-start | bytes 786440 | tf_op jit(solution)/shard_map/ppermute | solution.py:329
  320.2 21.2 %collective-permute-start.42 = (bf16[512,256]{1,0:T(8,128)(2,1)S(1)}, bf16[512,256]{1,0:T(8,128)(2,1)S(1)}, u32[]{:S(2)}, u32[]{:S(2)}) collective-permute-start(bf16[512,256]{1,0:T(8,128)(2,1)S(1)} %add.336), channel_id=1, source_target_pairs={{0,2},{2,0},{4,6},{6,4},{1,3},{3,1},{5,7},{7,5},{8,10},{10,8},{12,... | collective-permute-start | bytes 786440 | tf_op jit(solution)/shard_map/ppermute | solution.py:333
  327.0 14.6 %collective-permute-start.44 = (bf16[512,256]{1,0:T(8,128)(2,1)S(1)}, bf16[512,256]{1,0:T(8,128)(2,1)S(1)}, u32[]{:S(2)}, u32[]{:S(2)}) collective-permute-start(bf16[512,256]{1,0:T(8,128)(2,1)S(1)} %add.340), channel_id=1, source_target_pairs={{0,2},{2,0},{4,6},{6,4},{1,3},{3,1},{5,7},{7,5},{8,10},{10,8},{12,... | collective-permute-start | bytes 786440 | tf_op jit(solution)/shard_map/ppermute | solution.py:333
  330.1 1.6 collective-permute-start.45
  330.7 7.7 %collective-permute-start.47 = (bf16[512,256]{1,0:T(8,128)(2,1)S(1)}, bf16[512,256]{1,0:T(8,128)(2,1)S(1)}, u32[]{:S(2)}, u32[]{:S(2)}) collective-permute-start(bf16[512,256]{1,0:T(8,128)(2,1)S(1)} %add.341), channel_id=1, source_target_pairs={{2,4},{4,2},{3,5},{5,3},{10,12},{12,10},{11,13},{13,11},{18,20},{2... | collective-permute-start | bytes 786440 | tf_op jit(solution)/shard_map/ppermute | solution.py:329
  331.8 11.1 %collective-permute-start.46 = (bf16[512,256]{1,0:T(8,128)(2,1)S(1)}, bf16[512,256]{1,0:T(8,128)(2,1)S(1)}, u32[]{:S(2)}, u32[]{:S(2)}) collective-permute-start(bf16[512,256]{1,0:T(8,128)(2,1)S(1)} %add.344), channel_id=1, source_target_pairs={{0,2},{2,0},{4,6},{6,4},{1,3},{3,1},{5,7},{7,5},{8,10},{10,8},{12,... | collective-permute-start | bytes 786440 | tf_op jit(solution)/shard_map/ppermute | solution.py:333
  338.6 7.2 %collective-permute-start.48 = (bf16[512,256]{1,0:T(8,128)(2,1)S(1)}, bf16[512,256]{1,0:T(8,128)(2,1)S(1)}, u32[]{:S(2)}, u32[]{:S(2)}) collective-permute-start(bf16[512,256]{1,0:T(8,128)(2,1)S(1)} %add.347), channel_id=1, source_target_pairs={{0,2},{2,0},{4,6},{6,4},{1,3},{3,1},{5,7},{7,5},{8,10},{10,8},{12,... | collective-permute-start | bytes 786440 | tf_op jit(solution)/shard_map/ppermute | solution.py:333
  (12 other events, 257.3 us)
